TPU v7x, 128 devices: a whole 4x4x4 slice. The times are simulated.
128 devices in a mesh: ctx: 16 (over z, y_lo, core), fsdp: 8 (over x, y_hi).
Axes of the slice: x: 4, y: 4 (y_hi: 2, y_lo: 2; y = y_hi * 2 + y_lo), z: 4, core: 2. Of those that a mesh axis runs over, the one named last changes fastest.
Arguments:
- tokens: bfloat16 [8, 2, 16, 64, 2048], P('fsdp', None, 'ctx'), may hold values from -6 to 6
- gain_in: float32 [2048], replicated, may hold values from 0.5 to 1.5
- query_weight: bfloat16 [2048, 2048], P('fsdp'), may hold values from -0.125 to 0.125
- key_weight: bfloat16 [2048, 1024], P('fsdp'), may hold values from -0.125 to 0.125
- value_weight: bfloat16 [2048, 1024], P('fsdp'), may hold values from -0.125 to 0.125
- gain_query: float32 [128], replicated, may hold values from 0.5 to 1.5
- gain_key: float32 [128], replicated, may hold values from 0.5 to 1.5
- out_weight: bfloat16 [2048, 2048], P('fsdp'), may hold values from -4 to 4
- gain_mid: float32 [2048], replicated, may hold values from 0.5 to 1.5
- gate_weight: bfloat16 [2048, 6144], P('fsdp'), may hold values from -0.125 to 0.125
- up_weight: bfloat16 [2048, 6144], P('fsdp'), may hold values from -0.125 to 0.125
- down_weight: bfloat16 [6144, 2048], P('fsdp'), may hold values from -0.078125 to 0.078125
- cotangent: bfloat16 [8, 2, 16, 64, 2048], P('fsdp', None, 'ctx'), may hold values from -6 to 6
Outputs:
- mixed: bfloat16 [8, 2, 16, 64, 2048], P('fsdp', None, 'ctx')
- tokens_grad: bfloat16 [8, 2, 16, 64, 2048], P('fsdp', None, 'ctx')
- grad_gain_in: float32 [2048], replicated
- grad_query: float32 [2048, 2048], P(('ctx', 'fsdp'))
- grad_key: float32 [2048, 1024], P(('ctx', 'fsdp'))
- grad_value: float32 [2048, 1024], P(('ctx', 'fsdp'))
- grad_gain_query: float32 [128], replicated
- grad_gain_key: float32 [128], replicated
- grad_out: float32 [2048, 2048], P(('ctx', 'fsdp'))
- grad_gain_mid: float32 [2048], replicated
- grad_gate: float32 [2048, 6144], P(('ctx', 'fsdp'))
- grad_up: float32 [2048, 6144], P(('ctx', 'fsdp'))
- grad_down: float32 [6144, 2048], P(('ctx', 'fsdp'))
All inputs are finite; a program needn't handle non-finite values.
Results may differ from a plain program's by a relative error of at most 0.02.
Values may be sent and summed in bfloat16 or wider, within the bound.
A program may use at most 576 MiB of HBM per device.

v0:
```python
import jax
import jax.numpy as jnp
from jax import lax
from jax.sharding import PartitionSpec as P

EPS = 1e-06
THETA = 1000000.0


def rotary(positions, width):
    half = width // 2
    freq = THETA ** (-2.0 * jnp.arange(half, dtype=jnp.float32) / width)
    angle = positions.astype(jnp.float32)[:, None] * freq[None, :]
    cosine = jnp.concatenate([jnp.cos(angle), jnp.cos(angle)], 1)[:, None, :]
    sine = jnp.concatenate([jnp.sin(angle), jnp.sin(angle)], 1)[:, None, :]
    return (cosine, sine)


def turn(vals, cosine, sine):
    half = vals.shape[-1] // 2
    return vals * cosine + jnp.concatenate([-vals[..., half:], vals[..., :half]], -1) * sine


def turn_back(grads, cosine, sine):
    half = grads.shape[-1] // 2
    moved = grads * sine
    return grads * cosine + jnp.concatenate([moved[..., half:], -moved[..., :half]], -1)


def row_norm(vals):
    scale = lax.rsqrt(jnp.mean(vals * vals, -1, keepdims=True) + EPS)
    return (vals * scale, scale)


def norm_back(grad_unit, unit, scale):
    return scale * (grad_unit - unit * jnp.mean(grad_unit * unit, -1, keepdims=True))


def contract_cols(left, right):
    return lax.dot_general(
        left, right, (((1,), (1,)), ((), ())), preferred_element_type=jnp.float32
    )


def contract_rows(left, right):
    return lax.dot_general(
        left, right, (((0,), (0,)), ((), ())), preferred_element_type=jnp.float32
    )


def fold_rows(left, pieces):
    return tuple((jnp.dot(left, piece, preferred_element_type=jnp.float32) for piece in pieces))


def fold_back(grads, pieces):
    value = contract_cols(grads[0], pieces[0])
    for extra in range(1, len(pieces)):
        value = value + contract_cols(grads[extra], pieces[extra])
    return value


def shards(
    tokens,
    gain_in,
    query_weight,
    key_weight,
    value_weight,
    gain_query,
    gain_key,
    out_weight,
    gain_mid,
    gate_weight,
    up_weight,
    down_weight,
    cotangent,
):
    half = tokens.shape[3]
    width = tokens.shape[4]
    n_ctx = lax.axis_size("ctx")
    n_shard = lax.axis_size("fsdp")
    devices = n_ctx * n_shard
    rows = 2 * half
    head = gain_query.shape[0]
    kv_width = key_weight.shape[1]
    kv_heads = kv_width // head
    q_width = query_weight.shape[1]
    q_heads = q_width // head
    group = q_heads // kv_heads
    hidden = gate_weight.shape[1]
    factor = head ** (-0.5)
    here = lax.axis_index("ctx")
    local = jnp.arange(rows, dtype=jnp.int32)
    block = jnp.where(local // half == 0, here, 2 * n_ctx - 1 - here)
    query_pos = block * half + local % half
    everyone = jnp.arange(n_ctx * rows, dtype=jnp.int32)
    owner = everyone // rows
    spot = everyone % rows
    key_block = jnp.where(spot // half == 0, owner, 2 * n_ctx - 1 - owner)
    key_pos = key_block * half + spot % half
    allowed = key_pos[None, :] <= query_pos[:, None]
    cosine, sine = rotary(query_pos, head)
    x = tokens.reshape(rows, width).astype(jnp.float32)
    unit_in, scale_in = row_norm(x)
    h_b = (unit_in * gain_in).astype(jnp.bfloat16)
    q_raw, k_raw, v_raw = fold_rows(
        h_b,
        (
            lax.all_gather(query_weight, "fsdp", axis=0, tiled=True),
            lax.all_gather(key_weight, "fsdp", axis=0, tiled=True),
            lax.all_gather(value_weight, "fsdp", axis=0, tiled=True),
        ),
    )
    value_b = v_raw.astype(jnp.bfloat16)
    q_heads_raw = q_raw.reshape(rows, q_heads, head)
    k_heads_raw = k_raw.reshape(rows, kv_heads, head)
    unit_q, scale_q = row_norm(q_heads_raw)
    unit_k, scale_k = row_norm(k_heads_raw)
    query_b = turn(unit_q * gain_query, cosine, sine).astype(jnp.bfloat16)
    keys_b = turn(unit_k * gain_key, cosine, sine).astype(jnp.bfloat16).reshape(rows, kv_width)
    keys_all, values_all = (
        lax.all_gather(keys_b, "ctx", axis=0, tiled=True),
        lax.all_gather(value_b, "ctx", axis=0, tiled=True),
    )
    query_group = query_b.reshape(rows, kv_heads, group, head)

    def scores_of(key_rows):
        key_group = key_rows.reshape(-1, kv_heads, head)
        raw = (
            jnp.einsum("tgjd,sgd->gjts", query_group, key_group, preferred_element_type=jnp.float32)
            * factor
        )
        return jnp.where(allowed, raw, -1e30)

    scores = scores_of(keys_all)
    top = jnp.max(scores, -1, keepdims=True)
    expo = jnp.exp(scores - top)
    total = jnp.sum(expo, -1, keepdims=True)
    probs = expo / total
    log_total = top + jnp.log(total)
    attended = jnp.einsum(
        "gjts,sgd->tgjd",
        probs.astype(jnp.bfloat16),
        values_all.reshape(-1, kv_heads, head),
        preferred_element_type=jnp.float32,
    )
    attended = attended.reshape(rows, q_width).astype(jnp.bfloat16)
    (branch_out,) = fold_rows(attended, (lax.all_gather(out_weight, "fsdp", axis=0, tiled=True),))
    y_mid = x + branch_out
    unit_mid, scale_mid = row_norm(y_mid)
    h2_b = (unit_mid * gain_mid).astype(jnp.bfloat16)
    gate, upper = fold_rows(
        h2_b,
        (
            lax.all_gather(gate_weight, "fsdp", axis=0, tiled=True),
            lax.all_gather(up_weight, "fsdp", axis=0, tiled=True),
        ),
    )
    sig = jax.nn.sigmoid(gate)
    silu_gate = gate * sig
    act_b = (silu_gate * upper).astype(jnp.bfloat16)
    (branch_mlp,) = fold_rows(act_b, (lax.all_gather(down_weight, "fsdp", axis=0, tiled=True),))
    mixed = (y_mid + branch_mlp).astype(jnp.bfloat16).reshape(tokens.shape)
    grad_b = cotangent.reshape(rows, width)
    grad_f = grad_b.astype(jnp.float32)
    grad_act = contract_cols(grad_b, lax.all_gather(down_weight, "fsdp", axis=0, tiled=True))
    dgate_b = (grad_act * upper * sig * (1.0 + gate * (1.0 - sig))).astype(jnp.bfloat16)
    dup_b = (grad_act * silu_gate).astype(jnp.bfloat16)
    grad_h2 = fold_back(
        (dgate_b, dup_b),
        (
            lax.all_gather(gate_weight, "fsdp", axis=0, tiled=True),
            lax.all_gather(up_weight, "fsdp", axis=0, tiled=True),
        ),
    )
    term_mid = jnp.sum(grad_h2 * unit_mid, 0)
    grad_mid = grad_f + norm_back(grad_h2 * gain_mid, unit_mid, scale_mid)
    dz_b = grad_mid.astype(jnp.bfloat16)
    grad_att = contract_cols(dz_b, lax.all_gather(out_weight, "fsdp", axis=0, tiled=True))
    do_b = grad_att.astype(jnp.bfloat16).reshape(rows, kv_heads, group, head)
    keys_back, values_back = (
        lax.all_gather(keys_b, "ctx", axis=0, tiled=True),
        lax.all_gather(value_b, "ctx", axis=0, tiled=True),
    )
    probs_back = jnp.exp(scores_of(keys_back) - log_total)
    value_group = values_back.reshape(-1, kv_heads, head)
    grad_probs = jnp.einsum("tgjd,sgd->gjts", do_b, value_group, preferred_element_type=jnp.float32)
    delta = jnp.sum(probs_back * grad_probs, -1, keepdims=True)
    ds_b = (probs_back * (grad_probs - delta)).astype(jnp.bfloat16)
    grad_query = (
        jnp.einsum(
            "gjts,sgd->tgjd",
            ds_b,
            keys_back.reshape(-1, kv_heads, head),
            preferred_element_type=jnp.float32,
        )
        * factor
    )
    grad_keys = (
        jnp.einsum("gjts,tgjd->sgd", ds_b, query_group, preferred_element_type=jnp.float32) * factor
    )
    grad_values = jnp.einsum(
        "gjts,tgjd->sgd", probs_back.astype(jnp.bfloat16), do_b, preferred_element_type=jnp.float32
    )
    own_keys, own_values = (
        lax.psum_scatter(
            grad_keys.reshape(-1, kv_width).astype(jnp.bfloat16),
            "ctx",
            scatter_dimension=0,
            tiled=True,
        ).astype(jnp.float32),
        lax.psum_scatter(
            grad_values.reshape(-1, kv_width).astype(jnp.bfloat16),
            "ctx",
            scatter_dimension=0,
            tiled=True,
        ).astype(jnp.float32),
    )
    dv_b = own_values.astype(jnp.bfloat16)
    grad_q_turn = grad_query.astype(jnp.bfloat16).astype(jnp.float32).reshape(rows, q_heads, head)
    grad_k_turn = own_keys.astype(jnp.bfloat16).astype(jnp.float32).reshape(rows, kv_heads, head)
    grad_q_norm = turn_back(grad_q_turn, cosine, sine)
    grad_k_norm = turn_back(grad_k_turn, cosine, sine)
    term_query = jnp.sum(grad_q_norm * unit_q, (0, 1))
    term_key = jnp.sum(grad_k_norm * unit_k, (0, 1))
    dq_b = (
        norm_back(grad_q_norm * gain_query, unit_q, scale_q)
        .reshape(rows, q_width)
        .astype(jnp.bfloat16)
    )
    dk_b = (
        norm_back(grad_k_norm * gain_key, unit_k, scale_k)
        .reshape(rows, kv_width)
        .astype(jnp.bfloat16)
    )
    grad_h = fold_back(
        (dq_b, dk_b, dv_b),
        (
            lax.all_gather(query_weight, "fsdp", axis=0, tiled=True),
            lax.all_gather(key_weight, "fsdp", axis=0, tiled=True),
            lax.all_gather(value_weight, "fsdp", axis=0, tiled=True),
        ),
    )
    term_in = jnp.sum(grad_h * unit_in, 0)
    tokens_grad = (
        (grad_mid + norm_back(grad_h * gain_in, unit_in, scale_in))
        .astype(jnp.bfloat16)
        .reshape(tokens.shape)
    )
    edges = [
        0,
        q_width,
        q_width + kv_width,
        q_width + 2 * kv_width,
        q_width + 2 * kv_width + hidden,
        q_width + 2 * kv_width + 2 * hidden,
    ]
    ff_dev = hidden // devices
    qw_dev = q_width // devices
    late_rows = ff_dev + qw_dev
    blocks = late_rows * lax.axis_size(("ctx", "fsdp")) // late_rows
    down_part = contract_rows(act_b, grad_b).reshape(blocks, ff_dev, width)
    out_part = contract_rows(attended, dz_b).reshape(blocks, qw_dev, width)
    late = lax.psum_scatter(
        jnp.concatenate([down_part, out_part], 1).reshape(
            late_rows * lax.axis_size(("ctx", "fsdp")), width
        ),
        ("ctx", "fsdp"),
        scatter_dimension=0,
        tiled=True,
    )
    grad_down = late[:ff_dev]
    grad_out = late[ff_dev:]
    inner = lax.psum_scatter(
        jnp.concatenate(
            [
                contract_rows(h_b, dq_b),
                contract_rows(h_b, dk_b),
                contract_rows(h_b, dv_b),
                contract_rows(h2_b, dgate_b),
                contract_rows(h2_b, dup_b),
            ],
            1,
        ),
        ("ctx", "fsdp"),
        scatter_dimension=0,
        tiled=True,
    )
    grad_q_w = inner[:, edges[0] : edges[1]]
    grad_k_w = inner[:, edges[1] : edges[2]]
    grad_v_w = inner[:, edges[2] : edges[3]]
    grad_gate_w = inner[:, edges[3] : edges[4]]
    grad_up_w = inner[:, edges[4] : edges[5]]
    sum_in, sum_mid, sum_query, sum_key = lax.psum(
        (term_in, term_mid, term_query, term_key), ("ctx", "fsdp")
    )
    return (
        mixed,
        tokens_grad,
        sum_in,
        grad_q_w,
        grad_k_w,
        grad_v_w,
        sum_query,
        sum_key,
        grad_out,
        sum_mid,
        grad_gate_w,
        grad_up_w,
        grad_down,
    )


def solution(mesh):
    placed = (
        P("fsdp", None, "ctx", None, None),
        P(),
        P("fsdp", None),
        P("fsdp", None),
        P("fsdp", None),
        P(),
        P(),
        P("fsdp", None),
        P(),
        P("fsdp", None),
        P("fsdp", None),
        P("fsdp", None),
        P("fsdp", None, "ctx", None, None),
    )
    return jax.shard_map(
        shards,
        mesh=mesh,
        in_specs=placed,
        out_specs=(
            P("fsdp", None, "ctx", None, None),
            P("fsdp", None, "ctx", None, None),
            P(),
            P(("ctx", "fsdp"), None),
            P(("ctx", "fsdp"), None),
            P(("ctx", "fsdp"), None),
            P(),
            P(),
            P(("ctx", "fsdp"), None),
            P(),
            P(("ctx", "fsdp"), None),
            P(("ctx", "fsdp"), None),
            P(("ctx", "fsdp"), None),
        ),
        check_vma=False,
    )
```

profile of v0, /device:TPU:1, one launch (start us, length us, event | category | flops | bytes accessed | tf_op | source)
XLA Modules:
  0.0 5848.2 jit_solution(3166802032022125567)
XLA Ops:
  12.0 72.7 %all-gather.10.cloned.1.call-done = bf16[2048,1024]{1,0:T(8,128)(2,1)} async-done(((bf16[256,1024]{1,0:T(8,128)(2,1)}), bf16[2048,1024]{1,0:T(8,128)(2,1)}) %all-gather.10.cloned.1.call-update) | async-done | bytes 4194320 | tf_op jit(solution)/shard_map/all_gather | solution.py:110
  88.9 67.6 %all-gather.14.cloned.1.call-done = bf16[2048,1024]{1,0:T(8,128)(2,1)} async-done(((bf16[256,1024]{1,0:T(8,128)(2,1)}), bf16[2048,1024]{1,0:T(8,128)(2,1)}) %all-gather.14.cloned.1.call-update) | async-done | bytes 4194320 | tf_op jit(solution)/shard_map/all_gather | solution.py:109
  171.4 94.3 %all-gather.18.cloned.1.call-done = bf16[2048,2048]{1,0:T(8,128)(2,1)} async-done(((bf16[256,2048]{1,0:T(8,128)(2,1)}), bf16[2048,2048]{1,0:T(8,128)(2,1)}) %all-gather.18.cloned.1.call-update) | async-done | bytes 8388624 | tf_op jit(solution)/shard_map/all_gather | solution.py:108
  265.7 12.8 copy.66
  285.8 18.3 all-gather.12.cloned.1.call-done
  309.3 42.3 all-gather.16.cloned.1.call-done
  382.1 79.7 %all-gather.20.cloned.1.call-done = bf16[2048,2048]{1,0:T(8,128)(2,1)} async-done(((bf16[256,2048]{1,0:T(8,128)(2,1)}), bf16[2048,2048]{1,0:T(8,128)(2,1)}) %all-gather.20.cloned.1.call-update) | async-done | bytes 8388624 | tf_op jit(solution)/shard_map/all_gather | solution.py:147
  466.9 258.2 %all-gather.22.cloned.1.call-done = bf16[2048,6144]{1,0:T(8,128)(2,1)} async-done(((bf16[256,6144]{1,0:T(8,128)(2,1)}), bf16[2048,6144]{1,0:T(8,128)(2,1)}) %all-gather.22.cloned.1.call-update) | async-done | bytes 25165840 | tf_op jit(solution)/shard_map/all_gather | solution.py:154
  725.1 13.3 fusion.64
  738.4 249.9 %all-gather.24.cloned.1.call-done = bf16[2048,6144]{1,0:T(8,128)(2,1)} async-done(((bf16[256,6144]{1,0:T(8,128)(2,1)}), bf16[2048,6144]{1,0:T(8,128)(2,1)}) %all-gather.24.cloned.1.call-update) | async-done | bytes 25165840 | tf_op jit(solution)/shard_map/all_gather | solution.py:155
  988.3 15.2 fusion.15
  1003.5 248.1 %all-gather.26.cloned.1.call-done = bf16[6144,2048]{1,0:T(8,128)(2,1)} async-done(((bf16[768,2048]{1,0:T(8,128)(2,1)}), bf16[6144,2048]{1,0:T(8,128)(2,1)}) %all-gather.26.cloned.1.call-update) | async-done | bytes 25165840 | tf_op jit(solution)/shard_map/all_gather | solution.py:161
  1251.6 16.1 multiply_convert_fusion
  1267.7 14.7 fusion.65
  1282.3 15.3 multiply_reduce_fusion
  1306.1 12.8 fusion
  1318.9 11.8 fusion.2
  1369.8 20.8 fusion.21
  1390.6 43.8 pad_maximum_fusion
  1434.4 56.4 copy.83
  1519.2 21.2 convolution_dynamic-update-slice_fusion.1
  1540.4 21.0 convolution_dynamic-update-slice_fusion
  1569.0 14.8 fusion.20
  1587.1 4244.5 %all-reduce = (f32[2048]{0:T(1024)}, f32[128]{0:T(128)}, f32[128]{0:T(128)}, f32[2048]{0:T(1024)}) all-reduce(f32[2048]{0:T(1024)S(1)} %get-tuple-element.56, f32[128]{0:T(128)S(1)} %get-tuple-element.52, f32[128]{0:T(128)S(1)} %get-tuple-element.58, f32[2048]{0:T(1024)S(1)} %copy-done.40), channel_id=1, replica_groups=mesh['ctx'=16,'fsdp'=8] {'ctx','fsdp'}, use_global_device_ids=true, to_apply=%region_14.15 | all-reduce | flops 4352 | bytes 34816 | tf_op jit(solution)/shard_map/psum | solution.py:293
  (190 shorter events, 167.7 us)
Async XLA Ops:
  7.2 81.5 %copy-start.3 = (bf16[1,2,1,64,2048]{4,3,2,1,0:T(8,128)(2,1)S(1)}, bf16[1,2,1,64,2048]{4,3,2,1,0:T(8,128)(2,1)}, u32[]{:S(2)}) copy-start(bf16[1,2,1,64,2048]{4,3,2,1,0:T(8,128)(2,1)} %param.13) | copy-start | bytes 1572868
  7.2 81.5 %copy-start.35 = (f32[2048]{0:T(1024)S(1)}, f32[2048]{0:T(1024)}, u32[]{:S(2)}) copy-start(f32[2048]{0:T(1024)} %param.14) | copy-start | bytes 24580
  7.2 77.5 %all-gather.10.cloned.1.call-start = ((), (), s32[]{:S(2)}) async-start(), calls=%async_computation.4 | async-start | bytes 4718592 | tf_op jit(solution)/shard_map/all_gather | solution.py:110
  7.9 148.6 %all-gather.14.cloned.1.call-start = ((), (), s32[]{:S(2)}) async-start(), calls=%async_computation.6 | async-start | bytes 4718592 | tf_op jit(solution)/shard_map/all_gather | solution.py:109
  8.7 257.0 %all-gather.18.cloned.1.call-start = ((), (), s32[]{:S(2)}) async-start(), calls=%async_computation.8 | async-start | bytes 9437184 | tf_op jit(solution)/shard_map/all_gather | solution.py:108
  9.4 294.7 %all-gather.12.cloned.1.call-start = ((), (), s32[]{:S(2)}) async-start(), calls=%async_computation.5 | async-start | bytes 4456448 | tf_op jit(solution)/shard_map/all_gather | solution.py:122
  10.8 77.9 %copy-start.45 = (f32[128]{0:T(128)}, f32[128]{0:T(128)S(1)}, u32[]{:S(2)}) copy-start(f32[128]{0:T(128)S(1)} %rsqrt.37) | copy-start | bytes 1540
  88.3 78.2 %copy-start.41 = (f32[128]{0:T(128)S(1)}, f32[128]{0:T(128)}, u32[]{:S(2)}) copy-start(f32[128]{0:T(128)} %param.19) | copy-start | bytes 1540
  88.4 263.3 %all-gather.16.cloned.1.call-start = ((), (), s32[]{:S(2)}) async-start(), calls=%async_computation.7 | async-start | bytes 4456448 | tf_op jit(solution)/shard_map/all_gather | solution.py:121
  88.7 196.1 %copy-start.27 = (f32[128,128]{0,1:T(8,128)}, f32[128,128]{0,1:T(8,128)S(1)}, u32[]{:S(2)}) copy-start(f32[128,128]{0,1:T(8,128)S(1)} %get-tuple-element.97) | copy-start | bytes 196612
  88.7 196.1 %copy-start.30 = (f32[128,128]{0,1:T(8,128)}, f32[128,128]{0,1:T(8,128)S(1)}, u32[]{:S(2)}) copy-start(f32[128,128]{0,1:T(8,128)S(1)} %get-tuple-element.98) | copy-start | bytes 196612
  88.9 189.6 %copy-start.11 = (bf16[1,2,1,64,2048]{4,3,2,1,0:T(8,128)(2,1)}, bf16[1,2,1,64,2048]{4,3,2,1,0:T(8,128)(2,1)S(1)}, u32[]{:S(2)}) copy-start(bf16[1,2,1,64,2048]{4,3,2,1,0:T(8,128)(2,1)S(1)} %multiply_convert_fusion.6) | copy-start | bytes 1572868
  168.2 293.7 %all-gather.20.cloned.1.call-start = ((), (), s32[]{:S(2)}) async-start(), calls=%async_computation.9 | async-start | bytes 9437184 | tf_op jit(solution)/shard_map/all_gather | solution.py:147
  168.8 556.3 %all-gather.22.cloned.1.call-start = ((), (), s32[]{:S(2)}) async-start(), calls=%async_computation.10 | async-start | bytes 28311552 | tf_op jit(solution)/shard_map/all_gather | solution.py:154
  169.5 818.8 %all-gather.24.cloned.1.call-start = ((), (), s32[]{:S(2)}) async-start(), calls=%async_computation.11 | async-start | bytes 28311552 | tf_op jit(solution)/shard_map/all_gather | solution.py:155
  170.3 1081.3 %all-gather.26.cloned.1.call-start = ((), (), s32[]{:S(2)}) async-start(), calls=%async_computation.12 | async-start | bytes 28311552 | tf_op jit(solution)/shard_map/all_gather | solution.py:161
  171.0 1336.2 %reduce-scatter.13.cloned.1.call-start = ((), (), s32[]{:S(2)}) async-start(), calls=%async_computation.15 | async-start | bytes 4456448
  382.1 84.6 %copy-start.25 = (bf16[8,128,2,128]{3,1,2,0:T(8,128)(2,1)}, bf16[8,128,2,128]{3,1,2,0:T(8,128)(2,1)S(1)}, u32[]{:S(2)}) copy-start(bf16[8,128,2,128]{3,1,2,0:T(8,128)(2,1)S(1)} %fusion.25) | copy-start | bytes 1572868
  466.7 830.9 %copy-start.5 = (f32[128,2048]{1,0:T(8,128)}, f32[128,2048]{1,0:T(8,128)S(1)}, u32[]{:S(2)}) copy-start(f32[128,2048]{1,0:T(8,128)S(1)} %get-tuple-element.90) | copy-start | bytes 3145732
  466.9 521.5 %copy-start.20 = (bf16[128,2048]{1,0:T(8,128)(2,1)}, bf16[128,2048]{1,0:T(8,128)(2,1)S(1)}, u32[]{:S(2)}) copy-start(bf16[128,2048]{1,0:T(8,128)(2,1)S(1)} %multiply_convert_fusion.5) | copy-start | bytes 1572868
  1342.1 171.6 %reduce-scatter.15.cloned.1.call-start = ((), (), s32[]{:S(2)}) async-start(), calls=%async_computation.16 | async-start | bytes 4456448
  1359.5 4473.2 %reduce-scatter.11.cloned.1.call-start = ((), (), s32[]{:S(2)}) async-start(), calls=%async_computation.14 | async-start | bytes 67633152 | tf_op jit(solution)/shard_map/reduce_scatter | solution.py:263
  1490.9 4345.2 %reduce-scatter.9.cloned.1.call-start = ((), (), s32[]{:S(2)}) async-start(), calls=%async_computation.13 | async-start | bytes 135266304 | tf_op jit(solution)/shard_map/reduce_scatter | solution.py:273
  1583.8 4247.8 %copy-start.8 = (f32[128,2048]{1,0:T(8,128)S(1)}, f32[128,2048]{1,0:T(8,128)}, u32[]{:S(2)}) copy-start(f32[128,2048]{1,0:T(8,128)} %copy-done.7) | copy-start | bytes 3145732
  (36 other events, 489.8 us)
Sparse Core Ops, SparseCore 0:
  10.4 74.3 all-gather.9
  87.1 69.4 all-gather.13
  158.9 106.7 all-gather.17
  267.9 36.1 all-gather.11
  306.1 45.4 all-gather.15
  353.8 107.9 all-gather.19
  464.2 260.8 all-gather.21
  727.4 260.8 all-gather.23
  990.7 260.8 all-gather.25
  1342.2 66.0 reduce-scatter.12
  1410.7 68.8 reduce-scatter.14
  1490.9 1438.8 reduce-scatter.10
  2932.3 2869.4 reduce-scatter.8
where the time goes:
time: 5850 us
  blocking collectives  4240 us (72%)
  waiting for transfers between devices  1140 us (19%)
  matrix products  269 us (5%)
  local copies, waits for them, and re-layouts  109 us (2%)
  other arithmetic  73.6 us (1%)
    psum x1, blocking collectives, shards(): lax.psum((term_in, term_mid, term_query, term_key), ('ctx', 'fsdp'))  4240 us
    all_gather x1, waiting for transfers between devices, shards(): lax.all_gather(gate_weight, 'fsdp', axis=0, tiled=True)  258 us
    all_gather x1, waiting for transfers between devices, shards(): lax.all_gather(up_weight, 'fsdp', axis=0, tiled=True)  250 us
    all_gather x1, waiting for transfers between devices, shards(): lax.all_gather(down_weight, 'fsdp', axis=0, tiled=True)  248 us
  transfers between devices with their start and end apart: 13, of which 9 were waited for; matrix products, arithmetic and copies ran while one was open for 6% of the time, Pallas kernels for 0%

commit v1 on v0

v1 whole, which is shorter than its diff:
```python
import jax
import jax.numpy as jnp
from jax import lax
from jax.sharding import Mesh, PartitionSpec as P

EPS = 1e-06
THETA = 1000000.0
BF = jnp.bfloat16
F32 = jnp.float32
TP = ("z", "core")
FS = ("x", "yh")
DP = ("yl", "x", "yh")
ALL = ("z", "yl", "core", "x", "yh")


def rotary(positions, width):
    half = width // 2
    freq = THETA ** (-2.0 * jnp.arange(half, dtype=F32) / width)
    angle = positions.astype(F32)[:, None] * freq[None, :]
    cosine = jnp.concatenate([jnp.cos(angle), jnp.cos(angle)], 1)[:, None, :]
    sine = jnp.concatenate([jnp.sin(angle), jnp.sin(angle)], 1)[:, None, :]
    return (cosine, sine)


def turn(vals, cosine, sine):
    half = vals.shape[-1] // 2
    return vals * cosine + jnp.concatenate([-vals[..., half:], vals[..., :half]], -1) * sine


def turn_back(grads, cosine, sine):
    half = grads.shape[-1] // 2
    moved = grads * sine
    return grads * cosine + jnp.concatenate([moved[..., half:], -moved[..., :half]], -1)


def row_norm(vals):
    scale = lax.rsqrt(jnp.mean(vals * vals, -1, keepdims=True) + EPS)
    return (vals * scale, scale)


def norm_back(grad_unit, unit, scale):
    return scale * (grad_unit - unit * jnp.mean(grad_unit * unit, -1, keepdims=True))


def mm(left, right):
    return jnp.dot(left, right, preferred_element_type=F32)


def mm_t(left, right):
    return lax.dot_general(left, right, (((1,), (1,)), ((), ())), preferred_element_type=F32)


def t_mm(left, right):
    return lax.dot_general(left, right, (((0,), (0,)), ((), ())), preferred_element_type=F32)


def gather(val, axes):
    return lax.all_gather(val, axes, axis=0, tiled=True)


def scatter(val, axes):
    return lax.psum_scatter(val, axes, scatter_dimension=0, tiled=True)


def shards(
    tokens,
    gain_in,
    query_weight,
    key_weight,
    value_weight,
    gain_query,
    gain_key,
    out_weight,
    gain_mid,
    gate_weight,
    up_weight,
    down_weight,
    cotangent,
):
    half = tokens.shape[3]
    width = tokens.shape[4]
    n_z, n_yl, n_core = (lax.axis_size(a) for a in ("z", "yl", "core"))
    n_tp = n_z * n_core
    n_fs = lax.axis_size("x") * lax.axis_size("yh")
    n_ctx = n_tp * n_yl
    rows = 2 * half
    head = gain_query.shape[0]
    kv_width = key_weight.shape[1]
    q_width = query_weight.shape[1]
    hidden = gate_weight.shape[1]
    factor = head ** (-0.5)
    qc, kc, fc = q_width // n_tp, kv_width // n_tp, hidden // n_tp
    group = qc // head
    t = lax.axis_index(TP)
    yl = lax.axis_index("yl")

    def positions(lane):
        idx = jnp.arange(n_tp * rows, dtype=jnp.int32)
        who, spot = idx // rows, idx % rows
        c = (who // n_core) * (n_yl * n_core) + lane * n_core + who % n_core
        block = jnp.where(spot // half == 0, c, 2 * n_ctx - 1 - c)
        return block * half + spot % half

    query_pos = positions(yl)
    key_pos = jnp.concatenate([positions(i) for i in range(n_yl)])
    allowed = key_pos[None, :] <= query_pos[:, None]
    cosine, sine = rotary(query_pos, head)

    cut = lambda w, n: lax.dynamic_slice_in_dim(w, t * n, n, 1)
    w_qkv = gather(
        jnp.concatenate([cut(query_weight, qc), cut(key_weight, kc), cut(value_weight, kc)], 1), FS
    )
    w_gu = gather(jnp.concatenate([cut(gate_weight, fc), cut(up_weight, fc)], 1), FS)
    o_s, d_s = out_weight.shape[0] // n_tp, down_weight.shape[0] // n_tp
    rows_od = jnp.concatenate(
        [
            lax.dynamic_slice_in_dim(out_weight, t * o_s, o_s, 0),
            lax.dynamic_slice_in_dim(down_weight, t * d_s, d_s, 0),
        ],
        0,
    )
    rows_od = lax.ppermute(
        rows_od,
        TP + FS,
        [(a * n_fs + b, b * n_fs + a) for a in range(n_tp) for b in range(n_fs)],
    )
    w_od = gather(rows_od[None], FS)
    w_out = w_od[:, :o_s].reshape(n_fs * o_s, width)
    w_down = w_od[:, o_s:].reshape(n_fs * d_s, width)

    x = tokens.reshape(rows, width).astype(F32)
    unit_in, scale_in = row_norm(x)
    h = gather((unit_in * gain_in).astype(BF), TP)
    grad_l = cotangent.reshape(rows, width)
    g = gather(grad_l, TP)
    qkv = mm(h, w_qkv)
    value_b = qkv[:, qc + kc :].astype(BF)
    unit_q, scale_q = row_norm(qkv[:, :qc].reshape(-1, group, head))
    unit_k, scale_k = row_norm(qkv[:, qc : qc + kc].reshape(-1, 1, head))
    query_b = turn(unit_q * gain_query, cosine, sine).astype(BF)
    keys_b = turn(unit_k * gain_key, cosine, sine).astype(BF).reshape(-1, head)
    kv = gather(jnp.concatenate([keys_b, value_b], 1), ("yl",))
    keys, values = kv[:, :head], kv[:, head:]

    raw = jnp.einsum("tjd,sd->jts", query_b, keys, preferred_element_type=F32) * factor
    scores = jnp.where(allowed, raw, -1e30)
    top = jnp.max(scores, -1, keepdims=True)
    expo = jnp.exp(scores - top)
    probs = expo / jnp.sum(expo, -1, keepdims=True)
    probs_b = probs.astype(BF)
    attended = jnp.einsum("jts,sd->tjd", probs_b, values, preferred_element_type=F32)
    attended = attended.reshape(-1, qc).astype(BF)
    y_mid = x + scatter(mm(attended, w_out).astype(BF), TP).astype(F32)
    unit_mid, scale_mid = row_norm(y_mid)
    h2 = gather((unit_mid * gain_mid).astype(BF), TP)
    gu = mm(h2, w_gu)
    gate, upper = gu[:, :fc], gu[:, fc:]
    sig = jax.nn.sigmoid(gate)
    silu_gate = gate * sig
    act_b = (silu_gate * upper).astype(BF)
    mixed = (y_mid + scatter(mm(act_b, w_down).astype(BF), TP).astype(F32)).astype(BF)
    grad_act = mm_t(g, w_down)
    dgate_b = (grad_act * upper * sig * (1.0 + gate * (1.0 - sig))).astype(BF)
    dup_b = (grad_act * silu_gate).astype(BF)
    dgu = jnp.concatenate([dgate_b, dup_b], 1)
    grad_h2 = scatter(mm_t(dgu, w_gu).astype(BF), TP).astype(F32)
    term_mid = jnp.sum(grad_h2 * unit_mid, 0)
    grad_mid = grad_l.astype(F32) + norm_back(grad_h2 * gain_mid, unit_mid, scale_mid)
    dz = gather(grad_mid.astype(BF), TP)
    do_b = mm_t(dz, w_out).astype(BF).reshape(-1, group, head)
    grad_probs = jnp.einsum("tjd,sd->jts", do_b, values, preferred_element_type=F32)
    delta = jnp.sum(probs * grad_probs, -1, keepdims=True)
    ds_b = (probs * (grad_probs - delta)).astype(BF)
    grad_query = jnp.einsum("jts,sd->tjd", ds_b, keys, preferred_element_type=F32) * factor
    grad_keys = jnp.einsum("jts,tjd->sd", ds_b, query_b, preferred_element_type=F32) * factor
    grad_values = jnp.einsum("jts,tjd->sd", probs_b, do_b, preferred_element_type=F32)
    own = scatter(jnp.concatenate([grad_keys, grad_values], 1).astype(BF), ("yl",))
    dv_b = own[:, head:]
    grad_q_norm = turn_back(grad_query.astype(BF).astype(F32), cosine, sine)
    grad_k_norm = turn_back(own[:, :head].astype(F32).reshape(-1, 1, head), cosine, sine)
    term_query = jnp.sum(grad_q_norm * unit_q, (0, 1))
    term_key = jnp.sum(grad_k_norm * unit_k, (0, 1))
    dq_b = norm_back(grad_q_norm * gain_query, unit_q, scale_q).reshape(-1, qc).astype(BF)
    dk_b = norm_back(grad_k_norm * gain_key, unit_k, scale_k).reshape(-1, kc).astype(BF)
    dqkv = jnp.concatenate([dq_b, dk_b, dv_b], 1)
    grad_h = scatter(mm_t(dqkv, w_qkv).astype(BF), TP).astype(F32)
    term_in = jnp.sum(grad_h * unit_in, 0)
    tokens_grad = (grad_mid + norm_back(grad_h * gain_in, unit_in, scale_in)).astype(BF)

    def by_cols(part):
        cols = part.shape[1]
        part = part.astype(BF).reshape(n_z, n_yl, n_core, n_fs, -1, cols)
        part = part.transpose(1, 3, 0, 2, 4, 5).reshape(-1, cols)
        return scatter(part, DP)

    mine = jnp.concatenate([by_cols(t_mm(h2, dgu)), by_cols(t_mm(h, dqkv))], 1)
    mine = mine.reshape(n_tp, -1, mine.shape[1])
    mine = lax.all_to_all(mine, TP, 0, 0, tiled=True).transpose(1, 0, 2).astype(F32)

    def take(at, n):
        return mine[:, :, at : at + n].reshape(-1, n_tp * n)

    grad_gate_w, grad_up_w = take(0, fc), take(fc, fc)
    grad_q_w, grad_k_w, grad_v_w = (
        take(2 * fc, qc),
        take(2 * fc + qc, kc),
        take(2 * fc + qc + kc, kc),
    )
    blocks = n_yl * n_fs
    late = jnp.concatenate(
        [
            t_mm(act_b, g).astype(BF).reshape(blocks, -1, width),
            t_mm(attended, dz).astype(BF).reshape(blocks, -1, width),
        ],
        1,
    )
    ff_dev = fc // blocks
    late = scatter(late, DP)[0]
    late = lax.ppermute(
        late, ("yl", "core"), [(a * n_core + b, b * n_yl + a) for a in range(n_yl) for b in range(n_core)]
    ).astype(F32)
    grad_down, grad_out = late[:ff_dev], late[ff_dev:]
    sum_in, sum_mid, sum_query, sum_key = lax.psum((term_in, term_mid, term_query, term_key), ALL)
    return (
        mixed.reshape(tokens.shape),
        tokens_grad.reshape(tokens.shape),
        sum_in,
        grad_q_w,
        grad_k_w,
        grad_v_w,
        sum_query,
        sum_key,
        grad_out,
        sum_mid,
        grad_gate_w,
        grad_up_w,
        grad_down,
    )


def solution(mesh):
    fine = Mesh(mesh.devices.reshape(4, 2, 2, 4, 2), ALL)
    ctx, fsdp = ("z", "yl", "core"), FS
    act = P(fsdp, None, ctx, None, None)
    weight = P(fsdp, None)
    grad = P(ctx + fsdp, None)
    placed = (
        act, P(), weight, weight, weight, P(), P(), weight, P(), weight, weight, weight, act,
    )
    return jax.shard_map(
        shards,
        mesh=fine,
        in_specs=placed,
        out_specs=(act, act, P(), grad, grad, grad, P(), P(), grad, P(), grad, grad, grad),
        check_vma=False,
    )
```

time: 5850 us -> 1050 us (0.18)
  blocking collectives: 4240 us -> 95.5 us
  waiting for transfers between devices: 1140 us -> 724 us
  matrix products: 269 us -> 116 us
  local copies, waits for them, and re-layouts: 109 us -> 30.9 us
    psum x1, blocking collectives: 4240 us -> 68.6 us  [shards(): lax.psum((term_in, term_mid, term_query, term_key), ALL)]
    all_gather x9 -> x8, waiting for transfers between devices: 1130 us -> 328 us  [gather(): return lax.all_gather(val, axes, axis=0, tiled=True)]
    reduce_scatter x2 -> x8, waiting for transfers between devices: 0.01 us -> 362 us  [scatter(): return lax.psum_scatter(val, axes, scatter_dimension=0, tiled=True)]
    dot_general x27 -> x17, matrix products: 269 us -> 104 us  [the longest x4 27 us: mm_t(): lax.dot_general(left, right, (((1,), (1,)), ((), ())), preferred_element_...]
  transfers between devices with their start and end apart: 13 -> 18, of which waited for: 9 -> 16; matrix products, arithmetic and copies ran while one was open for 6% -> 10% of each run, Pallas kernels for 0% -> 0%
where the time goes in v1:
time: 1050 us; the launch traced here: 1040 us
  waiting for transfers between devices  724 us (69%)
  matrix products  116 us (11%)
  blocking collectives  95.5 us (9%)
  other arithmetic  45.1 us (4%)
  local copies, waits for them, and re-layouts  30.9 us (3%)
  between operations  15.2 us (1%)
  starting transfers between devices  14.6 us (1%)
    reduce_scatter x8, waiting for transfers between devices, scatter(): return lax.psum_scatter(val, axes, scatter_dimension=0, tiled=True)  362 us
    all_gather x8, waiting for transfers between devices, gather(): return lax.all_gather(val, axes, axis=0, tiled=True)  328 us
    psum x1, blocking collectives, shards(): lax.psum((term_in, term_mid, term_query, term_key), ALL)  68.6 us
    ppermute x1, waiting for transfers between devices, shards(): lax.ppermute(rows_od, TP + FS, [(a * n_fs + b, b * n_fs + a) for a in ran...  33 us
    dot_general x4, matrix products, mm_t(): lax.dot_general(left, right, (((1,), (1,)), ((), ())), preferred_element_...  27 us
    all_to_all x1, blocking collectives, shards(): lax.all_to_all(mine, TP, 0, 0, tiled=True).transpose(1, 0, 2).astype(F32)  26.9 us
    dot_general x4, matrix products, mm(): return jnp.dot(left, right, preferred_element_type=F32)  26.7 us
  transfers between devices with their start and end apart: 18, of which 16 were waited for; matrix products, arithmetic and copies ran while one was open for 10% of the time, Pallas kernels for 0%

profile of v1, /device:TPU:1, one launch (start us, length us, event | category | flops | bytes accessed | tf_op | source)
XLA Modules:
  0.0 1040.7 jit_solution(398500806890388429)
XLA Ops:
  20.7 33.0 %collective-permute-done = bf16[128,2048]{1,0:T(8,128)(2,1)S(1)} collective-permute-done((bf16[128,2048]{1,0:T(8,128)(2,1)S(1)}, bf16[128,2048]{1,0:T(8,128)(2,1)S(1)}, u32[]{:S(2)}, u32[]{:S(2)}) %collective-permute-start) | collective-permute-done | bytes 524320 | tf_op jit(solution)/shard_map/ppermute | solution.py:122
  58.8 32.2 %all-gather.12.cloned.1.call-done = bf16[2048,512]{1,0:T(8,128)(2,1)} async-done(((bf16[256,512]{1,0:T(8,128)(2,1)}), bf16[2048,512]{1,0:T(8,128)(2,1)}) %all-gather.12.cloned.1.call-update) | async-done | bytes 2097168 | tf_op jit(solution)/shard_map/all_gather | solution.py:58
  91.0 35.2 %all-gather.10.cloned.1.call-done = bf16[1024,2048]{1,0:T(8,128)(2,1)} async-done(((bf16[128,2048]{1,0:T(8,128)(2,1)}), bf16[1024,2048]{1,0:T(8,128)(2,1)}) %all-gather.10.cloned.1.call-update) | async-done | bytes 4194320 | tf_op jit(solution)/shard_map/all_gather | solution.py:58
  136.4 62.7 %all-gather.24.cloned.1.call-done = bf16[1024,2048]{1,0:T(8,128)(2,1)} async-done(((bf16[128,2048]{1,0:T(8,128)(2,1)}), bf16[1024,2048]{1,0:T(8,128)(2,1)}) %all-gather.24.cloned.1.call-update) | async-done | bytes 4194320 | tf_op jit(solution)/shard_map/all_gather | solution.py:58
  200.4 23.0 %all-gather.14.cloned.1.call-done = bf16[2048,256]{0,1:T(8,128)(2,1)} async-done(((bf16[1024,256]{0,1:T(8,128)(2,1)}), bf16[2048,256]{0,1:T(8,128)(2,1)}) %all-gather.14.cloned.1.call-update) | async-done | bytes 1048592 | tf_op jit(solution)/shard_map/all_gather | solution.py:58
  223.4 11.8 %fusion.91 = (f32[2,1024]{1,0:T(2,128)S(1)}, f32[2,1024,2048]{1,2,0:T(8,128)}) fusion(pred[1024,2048]{0,1:T(8,128)(4,1)} %broadcast_compare_fusion, bf16[1024,2,128]{0,2,1:T(8,128)(2,1)} %fusion.47, bf16[2048,256]{0,1:T(8,128)(2,1)} %all-gather.14.cloned.1.call-done), kind=kOutput, calls=%fused_computation.198 | convolution fusion | flops 1090521088 | bytes 19931136 | tf_op jit(solution)/shard_map/sub | solution.py:148
  248.4 33.6 %reduce-scatter.9.cloned.1.call-done = bf16[128,2048]{1,0:T(8,128)(2,1)} async-done(((bf16[1024,2048]{1,0:T(8,128)(2,1)}), bf16[128,2048]{1,0:T(8,128)(2,1)}) %reduce-scatter.9.cloned.1.call-update) | async-done | bytes 524304 | tf_op jit(solution)/shard_map/reduce_scatter | solution.py:62
  290.1 85.1 %all-gather.18.cloned.1.call-done = bf16[2048,1536]{1,0:T(8,128)(2,1)} async-done(((bf16[256,1536]{1,0:T(8,128)(2,1)}), bf16[2048,1536]{1,0:T(8,128)(2,1)}) %all-gather.18.cloned.1.call-update) | async-done | bytes 6291472 | tf_op jit(solution)/shard_map/all_gather | solution.py:58
  375.2 33.4 %all-gather.16.cloned.1.call-done = bf16[1024,2048]{1,0:T(8,128)(2,1)} async-done(((bf16[128,2048]{1,0:T(8,128)(2,1)}), bf16[1024,2048]{1,0:T(8,128)(2,1)}) %all-gather.16.cloned.1.call-update) | async-done | bytes 4194320 | tf_op jit(solution)/shard_map/all_gather | solution.py:58
  408.7 11.7 %fusion.93 = f32[1024,1536]{1,0:T(8,128)} fusion(bf16[1024,2048]{1,0:T(8,128)(2,1)} %all-gather.16.cloned.1.call-done, bf16[2048,1536]{1,0:T(8,128)(2,1)} %all-gather.18.cloned.1.call-done), kind=kOutput, calls=%fused_computation.200 | convolution fusion | flops 6442450944 | bytes 16777216 | tf_op jit(solution)/shard_map/dot_general | solution.py:46
  420.4 22.1 %all-gather.20.cloned.1.call-done = bf16[1024,2048]{1,0:T(8,128)(2,1)} async-done(((bf16[128,2048]{1,0:T(8,128)(2,1)}), bf16[1024,2048]{1,0:T(8,128)(2,1)}) %all-gather.20.cloned.1.call-update) | async-done | bytes 4194320 | tf_op jit(solution)/shard_map/all_gather | solution.py:58
  442.5 10.7 %fusion.14 = (bf16[1024,768]{1,0:T(8,128)(2,1)S(1)}, bf16[1024,768]{1,0:T(8,128)(2,1)S(1)}, bf16[1024,768]{1,0:T(8,128)(2,1)}) fusion(f32[1024,1536]{1,0:T(8,128)} %fusion.93, bf16[768,2048]{1,0:T(8,128)(2,1)} %bitcast.209, bf16[1024,2048]{1,0:T(8,128)(2,1)} %all-gather.20.cloned.1.call-done), kind=kOutput, calls=%fused_computation.30 | convolution fusion | flops 3233021952 | bytes 18350080 | tf_op jit(solution)/shard_map/dot_general | solution.py:50
  454.9 8.3 convolution_convert_fusion.1
  463.3 34.7 %reduce-scatter.13.cloned.1.call-done = bf16[128,2048]{1,0:T(8,128)(2,1)} async-done(((bf16[1024,2048]{1,0:T(8,128)(2,1)}), bf16[128,2048]{1,0:T(8,128)(2,1)}) %reduce-scatter.13.cloned.1.call-update) | async-done | bytes 524304 | tf_op jit(solution)/shard_map/reduce_scatter | solution.py:62
  502.7 34.3 %all-gather.22.cloned.1.call-done = bf16[1024,2048]{1,0:T(8,128)(2,1)} async-done(((bf16[128,2048]{1,0:T(8,128)(2,1)}), bf16[1024,2048]{1,0:T(8,128)(2,1)}) %all-gather.22.cloned.1.call-update) | async-done | bytes 4194320 | tf_op jit(solution)/shard_map/all_gather | solution.py:58
  540.7 8.8 fusion.21
  557.3 7.9 fusion.3
  569.8 9.5 convolution_convert_fusion
  625.8 108.8 %reduce-scatter.19.cloned.1.call-done = bf16[128,1536]{1,0:T(8,128)(2,1)} async-done(((bf16[2048,1536]{1,0:T(8,128)(2,1)}), bf16[128,1536]{1,0:T(8,128)(2,1)}) %reduce-scatter.19.cloned.1.call-update) | async-done | bytes 393232 | tf_op jit(solution)/shard_map/reduce_scatter | solution.py:62
  734.6 75.0 %reduce-scatter.21.cloned.1.call-done = bf16[128,512]{1,0:T(8,128)(2,1)} async-done(((bf16[2048,512]{1,0:T(8,128)(2,1)}), bf16[128,512]{1,0:T(8,128)(2,1)}) %reduce-scatter.21.cloned.1.call-update) | async-done | bytes 131088 | tf_op jit(solution)/shard_map/reduce_scatter | solution.py:62
  810.6 26.9 %all_to_all.5 = bf16[8,16,2048]{2,1,0:T(8,128)(2,1)S(1)} all-to-all(bf16[8,16,2048]{2,1,0:T(8,128)(2,1)S(1)} %bitcast.213), channel_id=1, replica_groups=mesh['z'=4,'yl'=2,'core'=2,'x'=4,'yh'=2] {'z','core'}, dimensions={0} | all-to-all | bytes 1048576 | tf_op jit(solution)/shard_map/all_to_all | solution.py:198
  838.6 78.5 %reduce-scatter.23.cloned.1.call-done = bf16[1,64,2048]{2,1,0:T(8,128)(2,1)} async-done(((bf16[16,64,2048]{2,1,0:T(8,128)(2,1)}), bf16[1,64,2048]{2,1,0:T(8,128)(2,1)}) %reduce-scatter.23.cloned.1.call-update) | async-done | bytes 262160 | tf_op jit(solution)/shard_map/reduce_scatter | solution.py:62
  930.7 29.2 %reduce-scatter.17.cloned.1.call-done = bf16[128,2048]{1,0:T(8,128)(2,1)} async-done(((bf16[1024,2048]{1,0:T(8,128)(2,1)}), bf16[128,2048]{1,0:T(8,128)(2,1)}) %reduce-scatter.17.cloned.1.call-update) | async-done | bytes 524304 | tf_op jit(solution)/shard_map/reduce_scatter | solution.py:62
  961.5 68.6 %all-reduce = (f32[2048]{0:T(1024)}, f32[128]{0:T(128)}, f32[128]{0:T(128)}, f32[2048]{0:T(1024)}) all-reduce(f32[2048]{0:T(1024)S(1)} %get-tuple-element.58, f32[128]{0:T(128)} %get-tuple-element.56, f32[128]{0:T(128)} %get-tuple-element.52, ...), channel_id=1, replica_groups=mesh['z'=4,'yl'=2,'core'=2,'x'=4,'yh'=2] {'z','yl','core','x','yh'}, use_global_device_ids=true, to_apply=%region_17.18 | all-reduce | flops 4352 | bytes 34816 | tf_op jit(solution)/shard_map/psum | solution.py:223
  (224 shorter events, 140.5 us)
Async XLA Ops:
  7.2 83.8 %all-gather.12.cloned.1.call-start = ((), (), s32[]{:S(2)}) async-start(), calls=%async_computation.10 | async-start | bytes 2359296 | tf_op jit(solution)/shard_map/all_gather | solution.py:58
  10.0 116.3 %all-gather.10.cloned.1.call-start = ((), (), s32[]{:S(2)}) async-start(), calls=%async_computation.9 | async-start | bytes 4718592 | tf_op jit(solution)/shard_map/all_gather | solution.py:58
  13.4 185.7 %all-gather.24.cloned.1.call-start = ((), (), s32[]{:S(2)}) async-start(), calls=%async_computation.24 | async-start | bytes 4718592 | tf_op jit(solution)/shard_map/all_gather | solution.py:58
  14.5 39.2 %collective-permute-start = (bf16[128,2048]{1,0:T(8,128)(2,1)S(1)}, bf16[128,2048]{1,0:T(8,128)(2,1)S(1)}, u32[]{:S(2)}, u32[]{:S(2)}) collective-permute-start(bf16[128,2048]{1,0:T(8,128)(2,1)S(1)} %pad_maximum_fusion.10), channel_id=1, source_target_pairs={{0,0},{1,8},{2,32},{3,40},{4,64},{5,72},{6,96},{7,104},{8,1},{9,9}... | collective-permute-start | bytes 1572872 | tf_op jit(solution)/shard_map/ppermute | solution.py:122
  54.5 168.9 %all-gather.14.cloned.1.call-start = ((), (), s32[]{:S(2)}) async-start(), calls=%async_computation.11 | async-start | bytes 1572864 | tf_op jit(solution)/shard_map/all_gather | solution.py:58
  56.4 75.4 %copy-start.12 = (f32[1024,64]{0,1:T(8,128)}, f32[1024,64]{0,1:T(8,128)S(1)}, u32[]{:S(2)}) copy-start(f32[1024,64]{0,1:T(8,128)S(1)} %get-tuple-element.85) | copy-start | bytes 786436
  58.8 72.8 %copy-start.34 = (f32[128]{0:T(128)S(1)}, f32[128]{0:T(128)}, u32[]{:S(2)}) copy-start(f32[128]{0:T(128)} %param.19) | copy-start | bytes 1540
  134.5 147.5 %reduce-scatter.9.cloned.1.call-start = ((), (), s32[]{:S(2)}) async-start(), calls=%async_computation.12 | async-start | bytes 4718592 | tf_op jit(solution)/shard_map/reduce_scatter | solution.py:62
  245.7 129.5 %all-gather.18.cloned.1.call-start = ((), (), s32[]{:S(2)}) async-start(), calls=%async_computation.14 | async-start | bytes 7077888 | tf_op jit(solution)/shard_map/all_gather | solution.py:58
  248.4 160.3 %all-gather.16.cloned.1.call-start = ((), (), s32[]{:S(2)}) async-start(), calls=%async_computation.13 | async-start | bytes 4718592 | tf_op jit(solution)/shard_map/all_gather | solution.py:58
  283.4 216.8 %copy-start.36 = (f32[128]{0:T(128)}, f32[128]{0:T(128)S(1)}, u32[]{:S(2)}) copy-start(f32[128]{0:T(128)S(1)} %add_rsqrt_fusion.3) | copy-start | bytes 1540
  285.4 157.1 %all-gather.20.cloned.1.call-start = ((), (), s32[]{:S(2)}) async-start(), calls=%async_computation.16 | async-start | bytes 4718592 | tf_op jit(solution)/shard_map/all_gather | solution.py:58
  286.2 211.8 %reduce-scatter.13.cloned.1.call-start = ((), (), s32[]{:S(2)}) async-start(), calls=%async_computation.17 | async-start | bytes 4718592 | tf_op jit(solution)/shard_map/reduce_scatter | solution.py:62
  463.2 73.8 %all-gather.22.cloned.1.call-start = ((), (), s32[]{:S(2)}) async-start(), calls=%async_computation.18 | async-start | bytes 4718592 | tf_op jit(solution)/shard_map/all_gather | solution.py:58
  502.4 89.7 %reduce-scatter.15.cloned.1.call-start = ((), (), s32[]{:S(2)}) async-start(), calls=%async_computation.19 | async-start | bytes 1572864 | tf_op jit(solution)/shard_map/reduce_scatter | solution.py:62
  569.7 164.8 %reduce-scatter.19.cloned.1.call-start = ((), (), s32[]{:S(2)}) async-start(), calls=%async_computation.21 | async-start | bytes 6684672 | tf_op jit(solution)/shard_map/reduce_scatter | solution.py:62
  582.5 227.0 %reduce-scatter.21.cloned.1.call-start = ((), (), s32[]{:S(2)}) async-start(), calls=%async_computation.22 | async-start | bytes 2228224 | tf_op jit(solution)/shard_map/reduce_scatter | solution.py:62
  600.9 316.1 %reduce-scatter.23.cloned.1.call-start = ((), (), s32[]{:S(2)}) async-start(), calls=%async_computation.23 | async-start | bytes 4456448 | tf_op jit(solution)/shard_map/reduce_scatter | solution.py:62
  611.2 348.7 %reduce-scatter.17.cloned.1.call-start = ((), (), s32[]{:S(2)}) async-start(), calls=%async_computation.20 | async-start | bytes 4718592 | tf_op jit(solution)/shard_map/reduce_scatter | solution.py:62
  617.5 412.6 %reduce-scatter.11.cloned.1.call-start = ((), (), s32[]{:S(2)}) async-start(), calls=%async_computation.15 | async-start | bytes 4718592 | tf_op jit(solution)/shard_map/reduce_scatter | solution.py:62
  810.6 149.3 %copy-start.33 = (f32[2048]{0:T(1024)S(1)}, f32[2048]{0:T(1024)}, u32[]{:S(2)}) copy-start(f32[2048]{0:T(1024)} %param.14) | copy-start | bytes 24580
  837.6 86.0 %copy-start.11 = (f32[16,8,2048]{2,0,1:T(8,128)}, f32[16,8,2048]{2,0,1:T(8,128)S(1)}, u32[]{:S(2)}) copy-start(f32[16,8,2048]{2,0,1:T(8,128)S(1)} %convert_bitcast_fusion) | copy-start | bytes 3145732
  917.0 12.2 %collective-permute-start.1 = (bf16[64,2048]{1,0:T(8,128)(2,1)}, bf16[64,2048]{1,0:T(8,128)(2,1)S(1)}, u32[]{:S(2)}, u32[]{:S(2)}) collective-permute-start(bf16[64,2048]{1,0:T(8,128)(2,1)} %bitcast.226), channel_id=1, source_target_pairs={{0,0},{8,16},{16,8},{24,24},{1,1},{9,17},{17,9},{25,25},{2,2},{10,... | collective-permute-start | bytes 786440 | tf_op jit(solution)/shard_map/ppermute | solution.py:219
  924.4 109.4 %copy-start.1 = (bf16[768,2048]{1,0:T(8,128)(2,1)S(1)}, bf16[768,2048]{1,0:T(8,128)(2,1)}, u32[]{:S(2)}) copy-start(bf16[768,2048]{1,0:T(8,128)(2,1)} %param.24) | copy-start | bytes 9437188
  (47 other events, 437.5 us)
Sparse Core Ops, SparseCore 0:
  10.9 80.0 all-gather.11
  93.3 32.9 all-gather.9
  128.6 70.4 all-gather.23
  201.2 22.1 all-gather.13
  245.8 36.1 reduce-scatter.8
  284.2 90.9 all-gather.17
  377.5 31.0 all-gather.15
  410.4 32.1 all-gather.19
  463.4 34.5 reduce-scatter.12
  502.6 34.4 all-gather.21
  569.8 22.2 reduce-scatter.14
  594.5 140.0 reduce-scatter.18
  737.1 72.4 reduce-scatter.20
  811.9 105.0 reduce-scatter.22
  919.4 40.4 reduce-scatter.16
  962.3 37.1 reduce-scatter.10

commit v2 on v1

--- a/solution.py
+++ b/solution.py
@@ -1,6 +1,10 @@
+import functools
+
 import jax
 import jax.numpy as jnp
 from jax import lax
+from jax.experimental import pallas as pl
+from jax.experimental.pallas import tpu as pltpu
 from jax.sharding import Mesh, PartitionSpec as P
 
 EPS = 1e-06
@@ -11,7 +15,125 @@
 FS = ("x", "yh")
 DP = ("yl", "x", "yh")
 ALL = ("z", "yl", "core", "x", "yh")
-
+MESH = pl.DeviceIdType.MESH
+VMEM = pl.BlockSpec(memory_space=pltpu.VMEM)
+HBM = pl.BlockSpec(memory_space=pl.ANY)
+MB = 2**20
+LOG2E = 1.4426950408889634
+
+
+class Place:
+    def __init__(self):
+        self.z, self.yl, self.core, self.x, self.yh = (lax.axis_index(a) for a in ALL)
+        self.t = 2 * self.z + self.core
+        self.shard = 2 * self.x + self.yh
+
+    def at(self, z=None, yl=None, core=None, x=None, yh=None):
+        here = (self.z, self.yl, self.core, self.x, self.yh)
+        return tuple(h if n is None else n for h, n in zip(here, (z, yl, core, x, yh)))
+
+    def up(self, n):
+        return lax.rem(self.z + n, 4)
+
+    def east(self, n):
+        return lax.rem(self.x + n, 4)
+
+    def peers(self, which):
+        table = {
+            "z": [self.at(z=self.up(1)), self.at(z=self.up(3))],
+            "sib": [self.at(core=1 - self.core)],
+            "x": [self.at(x=self.east(1)), self.at(x=self.east(3))],
+            "cross": [self.at(yl=1 - self.yl, yh=1 - self.yh)],
+            "pair": [self.at(yl=1 - self.yl)],
+            "tp": [
+                self.at(z=self.up(dz), core=lax.rem(self.core + dc, 2))
+                for dz in range(4)
+                for dc in range(2)
+                if dz or dc
+            ],
+        }
+        return [p for name in which for p in table[name]]
+
+
+class Wire:
+    def __init__(self, send_sem, recv_sem, here_sem):
+        self.send_sem, self.recv_sem, self.here_sem = send_sem, recv_sem, here_sem
+        self.n = self.m = 0
+        self.sent = []
+
+    def send(self, src, dst, peer):
+        copy = pltpu.make_async_remote_copy(
+            src_ref=src,
+            dst_ref=dst,
+            send_sem=self.send_sem.at[self.n],
+            recv_sem=self.recv_sem.at[self.n],
+            device_id=peer,
+            device_id_type=MESH,
+        )
+        self.n += 1
+        copy.start()
+        self.sent.append(copy)
+        return copy
+
+    def here(self, src, dst):
+        copy = pltpu.make_async_copy(src, dst, self.here_sem.at[self.m])
+        self.m += 1
+        copy.start()
+        return copy
+
+    def finish(self):
+        for copy in self.sent:
+            copy.wait_send()
+
+
+def sems(n, m):
+    return [
+        pltpu.SemaphoreType.DMA((n,)),
+        pltpu.SemaphoreType.DMA((n,)),
+        pltpu.SemaphoreType.DMA((m,)),
+    ]
+
+
+def meet(peers):
+    barrier = pltpu.get_barrier_semaphore()
+    for peer in peers:
+        pl.semaphore_signal(barrier, inc=1, device_id=peer, device_id_type=MESH)
+    pl.semaphore_wait(barrier, len(peers))
+
+
+def run(*tasks):
+    tasks = list(tasks)
+    while tasks:
+        advance(tasks)
+
+
+def advance(tasks):
+    for task in list(tasks):
+        try:
+            next(task)
+        except StopIteration:
+            tasks.remove(task)
+
+
+def swap_kernel(kv, far, send_sem, recv_sem, here_sem):
+    p = Place()
+    w = Wire(send_sem, recv_sem, here_sem)
+    meet(p.peers(("pair",)))
+    w.send(kv, far, p.at(yl=1 - p.yl)).wait()
+
+
+def swap(kv):
+    return pl.pallas_call(
+        swap_kernel,
+        out_shape=jax.ShapeDtypeStruct(kv.shape, kv.dtype),
+        in_specs=[VMEM],
+        out_specs=VMEM,
+        scratch_shapes=sems(1, 1),
+        compiler_params=pltpu.CompilerParams(
+            collective_id=0, has_side_effects=True, vmem_limit_bytes=16 * MB
+        ),
+        name="swap",
+    )(kv)
 
 def rotary(positions, width):
     half = width // 2
@@ -139,7 +261,9 @@
     unit_k, scale_k = row_norm(qkv[:, qc : qc + kc].reshape(-1, 1, head))
     query_b = turn(unit_q * gain_query, cosine, sine).astype(BF)
     keys_b = turn(unit_k * gain_key, cosine, sine).astype(BF).reshape(-1, head)
-    kv = gather(jnp.concatenate([keys_b, value_b], 1), ("yl",))
+    kv = jnp.concatenate([keys_b, value_b], 1)
+    kv_far = swap(kv)
+    kv = jnp.concatenate([jnp.where(yl == 0, kv, kv_far), jnp.where(yl == 0, kv_far, kv)])
     keys, values = kv[:, :head], kv[:, head:]
 
     raw = jnp.einsum("tjd,sd->jts", query_b, keys, preferred_element_type=F32) * factor

time: 1050 us -> 1010 us (0.962)
  waiting for transfers between devices: 724 us -> 652 us
  Pallas kernels: 0 us -> 14.6 us
    all_gather x8 -> x7, waiting for transfers between devices: 328 us -> 262 us  [gather(): return lax.all_gather(val, axes, axis=0, tiled=True)]
    pallas_call x0 -> x1, Pallas kernels: none -> 14.6 us  [swap(): pl.pallas_call(swap_kernel, out_shape=jax.ShapeDtypeStruct(kv.shape, kv.d...]
  transfers between devices with their start and end apart: 18 -> 17, of which waited for: 16 -> 15; matrix products, arithmetic and copies ran while one was open for 10% -> 13% of each run, Pallas kernels for 0% -> 1%
where the time goes in v2:
time: 1010 us; the launch traced here: 998 us
  waiting for transfers between devices  652 us (65%)
  matrix products  118 us (12%)
  blocking collectives  95.7 us (9%)
  other arithmetic  49.2 us (5%)
  local copies, waits for them, and re-layouts  39 us (4%)
  between operations  15.3 us (2%)
  Pallas kernels  14.6 us (1%)
  starting transfers between devices  14.3 us (1%)
    reduce_scatter x8, waiting for transfers between devices, scatter(): return lax.psum_scatter(val, axes, scatter_dimension=0, tiled=True)  356 us
    all_gather x7, waiting for transfers between devices, gather(): return lax.all_gather(val, axes, axis=0, tiled=True)  262 us
    psum x1, blocking collectives, shards(): lax.psum((term_in, term_mid, term_query, term_key), ALL)  68.6 us
    ppermute x1, waiting for transfers between devices, shards(): lax.ppermute(rows_od, TP + FS, [(a * n_fs + b, b * n_fs + a) for a in ran...  32.9 us
    all_to_all x1, blocking collectives, shards(): lax.all_to_all(mine, TP, 0, 0, tiled=True).transpose(1, 0, 2).astype(F32)  27.2 us
    dot_general x4, matrix products, mm_t(): lax.dot_general(left, right, (((1,), (1,)), ((), ())), preferred_element_...  27 us
    dot_general x4, matrix products, mm(): return jnp.dot(left, right, preferred_element_type=F32)  26.6 us
    dot_general x4, matrix products, t_mm(): lax.dot_general(left, right, (((0,), (0,)), ((), ())), preferred_element_...  21.7 us
  transfers between devices with their start and end apart: 17, of which 15 were waited for; matrix products, arithmetic and copies ran while one was open for 13% of the time, Pallas kernels for 1%

profile of v2, /device:TPU:1, one launch (start us, length us, event | category | flops | bytes accessed | tf_op | source)
XLA Modules:
  0.0 997.5 jit_solution(12823927317912409821)
XLA Ops:
  20.8 32.9 %collective-permute-done = bf16[128,2048]{1,0:T(8,128)(2,1)S(1)} collective-permute-done((bf16[128,2048]{1,0:T(8,128)(2,1)S(1)}, bf16[128,2048]{1,0:T(8,128)(2,1)S(1)}, u32[]{:S(2)}, u32[]{:S(2)}) %collective-permute-start) | collective-permute-done | bytes 524320 | tf_op jit(solution)/shard_map/ppermute | solution.py:244
  59.9 31.1 %all-gather.11.cloned.1.call-done = bf16[2048,512]{1,0:T(8,128)(2,1)} async-done(((bf16[256,512]{1,0:T(8,128)(2,1)}), bf16[2048,512]{1,0:T(8,128)(2,1)}) %all-gather.11.cloned.1.call-update) | async-done | bytes 2097168 | tf_op jit(solution)/shard_map/all_gather | solution.py:180
  91.0 35.2 %all-gather.9.cloned.1.call-done = bf16[1024,2048]{1,0:T(8,128)(2,1)} async-done(((bf16[128,2048]{1,0:T(8,128)(2,1)}), bf16[1024,2048]{1,0:T(8,128)(2,1)}) %all-gather.9.cloned.1.call-update) | async-done | bytes 4194320 | tf_op jit(solution)/shard_map/all_gather | solution.py:180
  143.3 14.6 %swap.1 = bf16[1024,256]{1,0:T(8,128)(2,1)S(1)} custom-call(bf16[1024,256]{1,0:T(8,128)(2,1)S(1)} %pad_maximum_fusion.10.kv), custom_call_target="tpu_custom_call" | custom-call | tf_op jit(solution)/shard_map/swap/pallas_call | solution.py:126
  159.8 12.0 %fusion.103 = (f32[2,1024]{1,0:T(2,128)S(1)}, f32[2,1024,2048]{1,2,0:T(8,128)}) fusion(pred[1024,2048]{0,1:T(8,128)(4,1)} %broadcast_compare_fusion, bf16[1024,2,128]{0,2,1:T(8,128)(2,1)S(1)} %fusion.47, bf16[1024,256]{1,0:T(8,128)(2,1)S(1)} %get-tuple-element.79, bf16[1024,256]{1,0:T(8,128)(2,1)} %get-tuple-element.80), kind=kOutput, calls=%fused_computation.203 | convolution fusion | flops 1091569664 | bytes 20455424 | tf_op jit(solution)/shard_map/sub | solution.py:272
  179.0 21.4 %all-gather.21.cloned.1.call-done = bf16[1024,2048]{1,0:T(8,128)(2,1)} async-done(((bf16[128,2048]{1,0:T(8,128)(2,1)}), bf16[1024,2048]{1,0:T(8,128)(2,1)}) %all-gather.21.cloned.1.call-update) | async-done | bytes 4194320 | tf_op jit(solution)/shard_map/all_gather | solution.py:180
  207.5 31.5 %reduce-scatter.9.cloned.1.call-done = bf16[128,2048]{1,0:T(8,128)(2,1)} async-done(((bf16[1024,2048]{1,0:T(8,128)(2,1)}), bf16[128,2048]{1,0:T(8,128)(2,1)}) %reduce-scatter.9.cloned.1.call-update) | async-done | bytes 524304 | tf_op jit(solution)/shard_map/reduce_scatter | solution.py:184
  247.1 84.9 %all-gather.15.cloned.1.call-done = bf16[2048,1536]{1,0:T(8,128)(2,1)} async-done(((bf16[256,1536]{1,0:T(8,128)(2,1)}), bf16[2048,1536]{1,0:T(8,128)(2,1)}) %all-gather.15.cloned.1.call-update) | async-done | bytes 6291472 | tf_op jit(solution)/shard_map/all_gather | solution.py:180
  331.9 32.7 %all-gather.13.cloned.1.call-done = bf16[1024,2048]{1,0:T(8,128)(2,1)} async-done(((bf16[128,2048]{1,0:T(8,128)(2,1)}), bf16[1024,2048]{1,0:T(8,128)(2,1)}) %all-gather.13.cloned.1.call-update) | async-done | bytes 4194320 | tf_op jit(solution)/shard_map/all_gather | solution.py:180
  364.6 11.7 %fusion.109 = f32[1024,1536]{1,0:T(8,128)} fusion(bf16[1024,2048]{1,0:T(8,128)(2,1)} %all-gather.13.cloned.1.call-done, bf16[2048,1536]{1,0:T(8,128)(2,1)} %all-gather.15.cloned.1.call-done), kind=kOutput, calls=%fused_computation.205 | convolution fusion | flops 6442450944 | bytes 16777216 | tf_op jit(solution)/shard_map/dot_general | solution.py:168
  376.3 22.2 %all-gather.17.cloned.1.call-done = bf16[1024,2048]{1,0:T(8,128)(2,1)} async-done(((bf16[128,2048]{1,0:T(8,128)(2,1)}), bf16[1024,2048]{1,0:T(8,128)(2,1)}) %all-gather.17.cloned.1.call-update) | async-done | bytes 4194320 | tf_op jit(solution)/shard_map/all_gather | solution.py:180
  398.5 10.7 %fusion.14 = (bf16[1024,768]{1,0:T(8,128)(2,1)S(1)}, bf16[1024,768]{1,0:T(8,128)(2,1)S(1)}, bf16[1024,768]{1,0:T(8,128)(2,1)}) fusion(f32[1024,1536]{1,0:T(8,128)} %fusion.109, bf16[768,2048]{1,0:T(8,128)(2,1)} %bitcast.207, bf16[1024,2048]{1,0:T(8,128)(2,1)} %all-gather.17.cloned.1.call-done), kind=kOutput, calls=%fused_computation.30 | convolution fusion | flops 3233021952 | bytes 18350080 | tf_op jit(solution)/shard_map/dot_general | solution.py:172
  410.9 8.3 convolution_convert_fusion.1
  419.2 34.7 %reduce-scatter.13.cloned.1.call-done = bf16[128,2048]{1,0:T(8,128)(2,1)} async-done(((bf16[1024,2048]{1,0:T(8,128)(2,1)}), bf16[128,2048]{1,0:T(8,128)(2,1)}) %reduce-scatter.13.cloned.1.call-update) | async-done | bytes 524304 | tf_op jit(solution)/shard_map/reduce_scatter | solution.py:184
  458.6 34.4 %all-gather.19.cloned.1.call-done = bf16[1024,2048]{1,0:T(8,128)(2,1)} async-done(((bf16[128,2048]{1,0:T(8,128)(2,1)}), bf16[1024,2048]{1,0:T(8,128)(2,1)}) %all-gather.19.cloned.1.call-update) | async-done | bytes 4194320 | tf_op jit(solution)/shard_map/all_gather | solution.py:180
  496.7 8.3 fusion.21
  513.8 7.9 fusion.3
  526.4 9.5 convolution_convert_fusion
  585.7 105.4 %reduce-scatter.19.cloned.1.call-done = bf16[128,1536]{1,0:T(8,128)(2,1)} async-done(((bf16[2048,1536]{1,0:T(8,128)(2,1)}), bf16[128,1536]{1,0:T(8,128)(2,1)}) %reduce-scatter.19.cloned.1.call-update) | async-done | bytes 393232 | tf_op jit(solution)/shard_map/reduce_scatter | solution.py:184
  691.1 75.1 %reduce-scatter.21.cloned.1.call-done = bf16[128,512]{1,0:T(8,128)(2,1)} async-done(((bf16[2048,512]{1,0:T(8,128)(2,1)}), bf16[128,512]{1,0:T(8,128)(2,1)}) %reduce-scatter.21.cloned.1.call-update) | async-done | bytes 131088 | tf_op jit(solution)/shard_map/reduce_scatter | solution.py:184
  767.4 27.2 %all_to_all.5 = bf16[8,16,2048]{2,1,0:T(8,128)(2,1)S(1)} all-to-all(bf16[8,16,2048]{2,1,0:T(8,128)(2,1)S(1)} %bitcast.211), channel_id=1, replica_groups=mesh['z'=4,'yl'=2,'core'=2,'x'=4,'yh'=2] {'z','core'}, dimensions={0} | all-to-all | bytes 1048576 | tf_op jit(solution)/shard_map/all_to_all | solution.py:322
  795.6 78.3 %reduce-scatter.23.cloned.1.call-done = bf16[1,64,2048]{2,1,0:T(8,128)(2,1)} async-done(((bf16[16,64,2048]{2,1,0:T(8,128)(2,1)}), bf16[1,64,2048]{2,1,0:T(8,128)(2,1)}) %reduce-scatter.23.cloned.1.call-update) | async-done | bytes 262160 | tf_op jit(solution)/shard_map/reduce_scatter | solution.py:184
  887.7 29.0 %reduce-scatter.17.cloned.1.call-done = bf16[128,2048]{1,0:T(8,128)(2,1)} async-done(((bf16[1024,2048]{1,0:T(8,128)(2,1)}), bf16[128,2048]{1,0:T(8,128)(2,1)}) %reduce-scatter.17.cloned.1.call-update) | async-done | bytes 524304 | tf_op jit(solution)/shard_map/reduce_scatter | solution.py:184
  918.3 68.6 %all-reduce = (f32[2048]{0:T(1024)}, f32[128]{0:T(128)}, f32[128]{0:T(128)}, f32[2048]{0:T(1024)}) all-reduce(f32[2048]{0:T(1024)S(1)} %get-tuple-element.58, f32[128]{0:T(128)} %get-tuple-element.54, f32[128]{0:T(128)} %get-tuple-element.56, ...), channel_id=1, replica_groups=mesh['z'=4,'yl'=2,'core'=2,'x'=4,'yh'=2] {'z','yl','core','x','yh'}, use_global_device_ids=true, to_apply=%region_17.18 | all-reduce | flops 4352 | bytes 34816 | tf_op jit(solution)/shard_map/psum | solution.py:347
  (232 shorter events, 154.9 us)
Async XLA Ops:
  7.2 83.8 %all-gather.11.cloned.1.call-start = ((), (), s32[]{:S(2)}) async-start(), calls=%async_computation.10 | async-start | bytes 2359296 | tf_op jit(solution)/shard_map/all_gather | solution.py:180
  10.0 116.3 %all-gather.9.cloned.1.call-start = ((), (), s32[]{:S(2)}) async-start(), calls=%async_computation.9 | async-start | bytes 4718592 | tf_op jit(solution)/shard_map/all_gather | solution.py:180
  11.3 120.1 %copy-start.41 = (f32[128]{0:T(128)}, f32[128]{0:T(128)S(1)}, u32[]{:S(2)}) copy-start(f32[128]{0:T(128)S(1)} %rsqrt.36) | copy-start | bytes 1540
  13.4 187.0 %all-gather.21.cloned.1.call-start = ((), (), s32[]{:S(2)}) async-start(), calls=%async_computation.23 | async-start | bytes 4718592 | tf_op jit(solution)/shard_map/all_gather | solution.py:180
  14.5 39.2 %collective-permute-start = (bf16[128,2048]{1,0:T(8,128)(2,1)S(1)}, bf16[128,2048]{1,0:T(8,128)(2,1)S(1)}, u32[]{:S(2)}, u32[]{:S(2)}) collective-permute-start(bf16[128,2048]{1,0:T(8,128)(2,1)S(1)} %pad_maximum_fusion.11), channel_id=1, source_target_pairs={{0,0},{1,8},{2,32},{3,40},{4,64},{5,72},{6,96},{7,104},{8,1},{9,9}... | collective-permute-start | bytes 1572872 | tf_op jit(solution)/shard_map/ppermute | solution.py:244
  54.5 184.4 %reduce-scatter.9.cloned.1.call-start = ((), (), s32[]{:S(2)}) async-start(), calls=%async_computation.11 | async-start | bytes 4718592 | tf_op jit(solution)/shard_map/reduce_scatter | solution.py:184
  57.5 77.7 %copy-start.10 = (f32[1024,64]{1,0:T(8,128)}, f32[1024,64]{1,0:T(8,128)S(1)}, u32[]{:S(2)}) copy-start(f32[1024,64]{1,0:T(8,128)S(1)} %get-tuple-element.89) | copy-start | bytes 786436
  59.9 74.9 %copy-start.36 = (f32[128]{0:T(128)S(1)}, f32[128]{0:T(128)}, u32[]{:S(2)}) copy-start(f32[128]{0:T(128)} %param.19) | copy-start | bytes 1540
  205.2 126.7 %all-gather.15.cloned.1.call-start = ((), (), s32[]{:S(2)}) async-start(), calls=%async_computation.13 | async-start | bytes 7077888 | tf_op jit(solution)/shard_map/all_gather | solution.py:180
  207.4 157.2 %all-gather.13.cloned.1.call-start = ((), (), s32[]{:S(2)}) async-start(), calls=%async_computation.12 | async-start | bytes 4718592 | tf_op jit(solution)/shard_map/all_gather | solution.py:180
  240.2 215.8 %copy-start.38 = (f32[128]{0:T(128)}, f32[128]{0:T(128)S(1)}, u32[]{:S(2)}) copy-start(f32[128]{0:T(128)S(1)} %add_rsqrt_fusion.3) | copy-start | bytes 1540
  242.3 156.2 %all-gather.17.cloned.1.call-start = ((), (), s32[]{:S(2)}) async-start(), calls=%async_computation.15 | async-start | bytes 4718592 | tf_op jit(solution)/shard_map/all_gather | solution.py:180
  243.1 210.8 %reduce-scatter.13.cloned.1.call-start = ((), (), s32[]{:S(2)}) async-start(), calls=%async_computation.16 | async-start | bytes 4718592 | tf_op jit(solution)/shard_map/reduce_scatter | solution.py:184
  419.2 73.8 %all-gather.19.cloned.1.call-start = ((), (), s32[]{:S(2)}) async-start(), calls=%async_computation.17 | async-start | bytes 4718592 | tf_op jit(solution)/shard_map/all_gather | solution.py:180
  458.4 90.2 %reduce-scatter.15.cloned.1.call-start = ((), (), s32[]{:S(2)}) async-start(), calls=%async_computation.18 | async-start | bytes 1572864 | tf_op jit(solution)/shard_map/reduce_scatter | solution.py:184
  526.2 164.9 %reduce-scatter.19.cloned.1.call-start = ((), (), s32[]{:S(2)}) async-start(), calls=%async_computation.20 | async-start | bytes 6684672 | tf_op jit(solution)/shard_map/reduce_scatter | solution.py:184
  539.2 227.0 %reduce-scatter.21.cloned.1.call-start = ((), (), s32[]{:S(2)}) async-start(), calls=%async_computation.21 | async-start | bytes 2228224 | tf_op jit(solution)/shard_map/reduce_scatter | solution.py:184
  560.7 313.1 %reduce-scatter.23.cloned.1.call-start = ((), (), s32[]{:S(2)}) async-start(), calls=%async_computation.22 | async-start | bytes 4456448 | tf_op jit(solution)/shard_map/reduce_scatter | solution.py:184
  571.2 345.4 %reduce-scatter.17.cloned.1.call-start = ((), (), s32[]{:S(2)}) async-start(), calls=%async_computation.19 | async-start | bytes 4718592 | tf_op jit(solution)/shard_map/reduce_scatter | solution.py:184
  577.5 409.4 %reduce-scatter.11.cloned.1.call-start = ((), (), s32[]{:S(2)}) async-start(), calls=%async_computation.14 | async-start | bytes 4718592 | tf_op jit(solution)/shard_map/reduce_scatter | solution.py:184
  767.3 149.3 %copy-start.35 = (f32[2048]{0:T(1024)S(1)}, f32[2048]{0:T(1024)}, u32[]{:S(2)}) copy-start(f32[2048]{0:T(1024)} %param.14) | copy-start | bytes 24580
  794.6 86.0 %copy-start.14 = (f32[16,8,2048]{2,0,1:T(8,128)}, f32[16,8,2048]{2,0,1:T(8,128)S(1)}, u32[]{:S(2)}) copy-start(f32[16,8,2048]{2,0,1:T(8,128)S(1)} %convert_bitcast_fusion) | copy-start | bytes 3145732
  873.8 12.4 %collective-permute-start.1 = (bf16[64,2048]{1,0:T(8,128)(2,1)}, bf16[64,2048]{1,0:T(8,128)(2,1)S(1)}, u32[]{:S(2)}, u32[]{:S(2)}) collective-permute-start(bf16[64,2048]{1,0:T(8,128)(2,1)} %bitcast.224), channel_id=1, source_target_pairs={{0,0},{8,16},{16,8},{24,24},{1,1},{9,17},{17,9},{25,25},{2,2},{10,... | collective-permute-start | bytes 786440 | tf_op jit(solution)/shard_map/ppermute | solution.py:343
  881.4 109.2 %copy-start.1 = (bf16[768,2048]{1,0:T(8,128)(2,1)S(1)}, bf16[768,2048]{1,0:T(8,128)(2,1)}, u32[]{:S(2)}) copy-start(bf16[768,2048]{1,0:T(8,128)(2,1)} %param.24) | copy-start | bytes 9437188
  (47 other events, 511.8 us)
Sparse Core Ops, SparseCore 0:
  10.9 80.0 all-gather.10
  93.3 32.9 all-gather.8
  128.6 71.8 all-gather.20
  205.3 33.5 reduce-scatter.8
  241.1 90.7 all-gather.14
  333.5 31.0 all-gather.12
  366.3 32.1 all-gather.16
  419.3 34.5 reduce-scatter.12
  458.5 34.4 all-gather.18
  526.3 22.2 reduce-scatter.14
  551.1 139.9 reduce-scatter.18
  693.5 72.7 reduce-scatter.20
  768.8 105.0 reduce-scatter.22
  876.2 40.3 reduce-scatter.16
  919.0 37.3 reduce-scatter.10

commit v3 on v2

v3 whole, which is shorter than its diff:
```python
import functools

import jax
import jax.numpy as jnp
from jax import lax
from jax.experimental import pallas as pl
from jax.experimental.pallas import tpu as pltpu
from jax.sharding import Mesh, PartitionSpec as P

EPS = 1e-06
THETA = 1000000.0
BF = jnp.bfloat16
F32 = jnp.float32
TP = ("z", "core")
FS = ("x", "yh")
DP = ("yl", "x", "yh")
ALL = ("z", "yl", "core", "x", "yh")
MESH = pl.DeviceIdType.MESH
VMEM = pl.BlockSpec(memory_space=pltpu.VMEM)
HBM = pl.BlockSpec(memory_space=pl.ANY)
MB = 2**20
LOG2E = 1.4426950408889634


class Place:
    def __init__(self):
        self.z, self.yl, self.core, self.x, self.yh = (lax.axis_index(a) for a in ALL)
        self.t = 2 * self.z + self.core
        self.shard = 2 * self.x + self.yh
        self.y = 2 * self.yh + self.yl

    def at(self, z=None, yl=None, core=None, x=None, yh=None):
        here = (self.z, self.yl, self.core, self.x, self.yh)
        return tuple(h if n is None else n for h, n in zip(here, (z, yl, core, x, yh)))

    def up(self, n):
        return lax.rem(self.z + n, 4)

    def east(self, n):
        return lax.rem(self.x + n, 4)

    def north(self, n):
        y = lax.rem(self.y + n, 4)
        return self.at(yh=y // 2, yl=lax.rem(y, 2))

    def peers(self, which):
        table = {
            "z": [self.at(z=self.up(1)), self.at(z=self.up(3))],
            "sib": [self.at(core=1 - self.core)],
            "x": [self.at(x=self.east(1)), self.at(x=self.east(3))],
            "cross": [self.at(yl=1 - self.yl, yh=1 - self.yh)],
            "pair": [self.at(yl=1 - self.yl)],
            "plane": [self.at(x=self.east(d)) for d in (1, 2, 3)]
            + [self.north(d) for d in (1, 2, 3)],
            "swap": [self.at(yl=1 - self.yl, core=1 - self.core)],
            "tp": [
                self.at(z=self.up(dz), core=lax.rem(self.core + dc, 2))
                for dz in range(4)
                for dc in range(2)
                if dz or dc
            ],
        }
        return [p for name in which for p in table[name]]


class Wire:
    def __init__(self, send_sem, recv_sem, here_sem):
        self.send_sem, self.recv_sem, self.here_sem = send_sem, recv_sem, here_sem
        self.n = self.m = 0
        self.sent = []

    def send(self, src, dst, peer):
        copy = pltpu.make_async_remote_copy(
            src_ref=src,
            dst_ref=dst,
            send_sem=self.send_sem.at[self.n],
            recv_sem=self.recv_sem.at[self.n],
            device_id=peer,
            device_id_type=MESH,
        )
        self.n += 1
        copy.start()
        self.sent.append(copy)
        return copy

    def here(self, src, dst):
        copy = pltpu.make_async_copy(src, dst, self.here_sem.at[self.m])
        self.m += 1
        copy.start()
        return copy

    def finish(self):
        for copy in self.sent:
            copy.wait_send()


def sems(n, m):
    return [
        pltpu.SemaphoreType.DMA((n,)),
        pltpu.SemaphoreType.DMA((n,)),
        pltpu.SemaphoreType.DMA((m,)),
    ]


def meet(peers):
    barrier = pltpu.get_barrier_semaphore()
    for peer in peers:
        pl.semaphore_signal(barrier, inc=1, device_id=peer, device_id_type=MESH)
    pl.semaphore_wait(barrier, len(peers))


def run(*tasks):
    tasks = list(tasks)
    while tasks:
        advance(tasks)


def advance(tasks):
    for task in list(tasks):
        try:
            next(task)
        except StopIteration:
            tasks.remove(task)


def gather_z(w, p, own, dst):
    up, down, sib = p.at(z=p.up(1)), p.at(z=p.up(3)), p.at(core=1 - p.core)
    before, after, far = (2 * p.up(n) + p.core for n in (3, 1, 2))
    u0 = w.send(own(0), dst(p.t, 0), up)
    d1 = w.send(own(1), dst(p.t, 1), down)
    u1 = w.send(own(1), dst(p.t, 1), up)
    d0 = w.send(own(0), dst(p.t, 0), down)
    s = [w.send(own(k), dst(p.t, k), sib) for k in (0, 1)]

    def on(t, k):
        s.append(w.send(dst(t, k), dst(t, k), sib))

    yield
    u0.wait_recv()
    f0 = w.send(dst(before, 0), dst(before, 0), up)
    on(before, 0)
    d1.wait_recv()
    f1 = w.send(dst(after, 1), dst(after, 1), down)
    on(after, 1)
    yield
    u1.wait_recv()
    on(before, 1)
    d0.wait_recv()
    on(after, 0)
    yield
    f0.wait_recv()
    on(far, 0)
    f1.wait_recv()
    on(far, 1)
    yield
    for copy in s:
        copy.wait_recv()


def gather_xy(w, p, own, dst, n, ready=None):
    east, west = p.at(x=p.east(1)), p.at(x=p.east(3))
    cross, pair = p.at(yl=1 - p.yl, yh=1 - p.yh), p.at(yl=1 - p.yl)
    half = n // 2
    west_s, east_s, far_s = (2 * p.east(k) + p.yh for k in (3, 1, 2))
    mine = p.yl * half
    other = half - mine
    flip = 1 - 2 * p.yh

    def over(s):
        return w.send(dst(s, mine, half), dst(s, mine, half), cross)

    def along(s):
        return w.send(dst(s + flip, other, half), dst(s + flip, other, half), pair)

    e0 = w.send(own(0, half), dst(p.shard, 0, half), east)
    w1 = w.send(own(half, half), dst(p.shard, half, half), west)
    c0 = w.send(own(mine, half), dst(p.shard, mine, half), cross)
    e1 = w.send(own(half, half), dst(p.shard, half, half), east)
    w0 = w.send(own(0, half), dst(p.shard, 0, half), west)
    yield
    e0.wait_recv()
    f0 = w.send(dst(west_s, 0, half), dst(west_s, 0, half), east)
    w1.wait_recv()
    f1 = w.send(dst(east_s, half, half), dst(east_s, half, half), west)
    yield
    c0.wait_recv()
    a0 = along(p.shard)
    e1.wait_recv()
    c1 = over(west_s)
    w0.wait_recv()
    c2 = over(east_s)
    if ready:
        ready(west_s)
        ready(east_s)
    yield
    f0.wait_recv()
    f1.wait_recv()
    c3 = over(far_s)
    if ready:
        ready(far_s)
    yield
    c1.wait_recv()
    a1 = along(west_s)
    c2.wait_recv()
    a2 = along(east_s)
    yield
    c3.wait_recv()
    a3 = along(far_s)
    yield
    for s, a in ((p.shard, a0), (west_s, a1), (east_s, a2), (far_s, a3)):
        a.wait_recv()
        if ready:
            ready(s + flip)


def norm_rope(raw, gain, cosine, sine):
    unit = raw * lax.rsqrt(jnp.mean(raw * raw, -1, keepdims=True) + EPS)
    vals = unit * gain
    return vals * cosine + pltpu.roll(vals, 64, 1) * sine


def front_kernel(
    tok, gain, w_own, cosine, sine, gq, gk, h, w_qkv, q, kv, raw, send_sem, recv_sem, here_sem
):
    p = Place()
    w = Wire(send_sem, recv_sem, here_sem)
    w_qkv[pl.ds(pl.multiple_of(p.shard * 256, 256), 256)] = w_own[...]
    for k in (0, 1):
        x = tok[k].astype(F32)
        unit = x * lax.rsqrt(jnp.mean(x * x, -1, keepdims=True) + EPS)
        h[p.t if k == 0 else 15 - p.t] = (unit * gain[...]).astype(BF)
    meet(p.peers(("z", "sib", "x", "cross", "pair")))

    def block(t, k):
        return h.at[t if k == 0 else 15 - t]

    def part(s, at, n):
        return w_qkv.at[pl.ds(pl.multiple_of(s * 256 + at, 128), n)]

    run(
        gather_z(w, p, lambda k: block(p.t, k), block),
        gather_xy(w, p, lambda at, n: part(p.shard, at, n), part, 256),
    )

    @pl.loop(0, 4)
    def _(j):
        at = pl.ds(pl.multiple_of(j * 256, 256), 256)
        rows_h = h[pl.ds(4 * j, 4)].reshape(256, 2048)
        out = jnp.dot(rows_h, w_qkv[...], preferred_element_type=F32)
        cos, sin = cosine[at], sine[at]
        raw[at] = out[:, :384]
        for n in (0, 1):
            cols = slice(n * 128, n * 128 + 128)
            q[at, cols] = norm_rope(out[:, cols], gq[...], cos, sin).astype(BF)
        kv[at, 0:128] = norm_rope(out[:, 256:384], gk[...], cos, sin).astype(BF)
        kv[at, 128:256] = out[:, 384:].astype(BF)

    w.finish()


def front(tok, gain, w_own, cosine, sine, gq, gk):
    sds = jax.ShapeDtypeStruct
    return pl.pallas_call(
        front_kernel,
        out_shape=(
            sds((16, 64, 2048), BF),
            sds((2048, 512), BF),
            sds((1024, 256), BF),
            sds((1024, 256), BF),
            sds((1024, 384), F32),
        ),
        in_specs=[VMEM] * 7,
        out_specs=[VMEM] * 5,
        scratch_shapes=sems(48, 4),
        compiler_params=pltpu.CompilerParams(
            collective_id=0, has_side_effects=True, vmem_limit_bytes=48 * MB
        ),
        name="front",
    )(tok, gain, w_own, cosine, sine, gq, gk)


SCALE = 128**-0.5 * LOG2E


def dot_t(a, b):
    return lax.dot_general(a, b, (((1,), (1,)), ((), ())), preferred_element_type=F32)


def t_dot(a, b):
    return lax.dot_general(a, b, (((0,), (0,)), ((), ())), preferred_element_type=F32)


def both(ref, at):
    return jnp.concatenate([ref[at, 0:128], ref[at, 128:256]], 0)


def weights_of(q, k, j, edge):
    s = jnp.exp2(dot_t(q, k) * SCALE)
    last = jnp.where(edge, s[:, j * 128 :], 0.0)
    return last if j == 0 else jnp.concatenate([s[:, : j * 128], last], 1)


def edges(p, j):
    row = lax.broadcasted_iota(jnp.int32, (256, 128), 0) % 128
    col = lax.broadcasted_iota(jnp.int32, (256, 128), 1)
    seen = (p.yl if j < 4 else 1 - p.yl) * 128
    return col <= row, col < seen


def attend_kernel(
    q, kv, cot, wo, gu_own, o, o_tok, kv_far, g, w_out, w_gu, send_sem, recv_sem, here_sem
):
    p = Place()
    w = Wire(send_sem, recv_sem, here_sem)
    g[p.t] = cot[0]
    g[15 - p.t] = cot[1]
    w_out[p.shard, p.core] = wo[...]
    w_gu[p.shard] = gu_own[...]
    meet(p.peers(("tp", "x", "cross", "pair")))
    swap = w.send(kv, kv_far, p.at(yl=1 - p.yl))

    def block(t, k):
        return g.at[t if k == 0 else 15 - t]

    def part(s, at, n):
        return w_out.at[s, p.core, pl.ds(pl.multiple_of(at, 64), n)]

    twin = []

    def ready(s):
        twin.append(
            w.send(w_out.at[s, p.core], w_out.at[s, p.core], p.at(core=1 - p.core))
        )

    ready(p.shard)

    def part_gu(s, at, n):
        return w_gu.at[s, pl.ds(pl.multiple_of(at, 128), n)]

    tasks = [
        gather_z(w, p, lambda k: block(p.t, k), block),
        gather_xy(w, p, lambda at, n: part(p.shard, at, n), part, 128, ready),
        gather_xy(w, p, lambda at, n: part_gu(p.shard, at, n), part_gu, 256),
    ]
    advance(tasks)
    swap.wait_recv()
    spread = []
    mine = pl.ds(pl.multiple_of(p.t * 256, 256), 256)
    for j in range(8):
        at = pl.ds(j * 128, 128)
        keys = pl.ds(0, j * 128 + 128)
        tri, seen = edges(p, j)
        qj = both(q, at)
        near = weights_of(qj, kv[keys, 0:128], j, tri)
        far = weights_of(qj, kv_far[keys, 0:128], j, seen)
        total = jnp.sum(near, -1, keepdims=True) + jnp.sum(far, -1, keepdims=True)
        out = jnp.dot(near.astype(BF), kv[keys, 128:256], preferred_element_type=F32)
        out += jnp.dot(far.astype(BF), kv_far[keys, 128:256], preferred_element_type=F32)
        out = (out / total).astype(BF)
        for n in (0, 1):
            o[2 * j : 2 * j + 2, :, n * 128 : n * 128 + 128] = out[
                n * 128 : n * 128 + 128
            ].reshape(2, 64, 128)
        advance(tasks)
    run(*tasks)
    for dz in range(4):
        for dc in range(2):
            z, core = p.up(dz), lax.rem(p.core + dc, 2)
            t = 2 * z + core
            for k in (0, 1):
                src = o.at[t if k == 0 else 15 - t]
                dst = o_tok.at[k, :, mine]
                if dz or dc:
                    spread.append(w.send(src, dst, p.at(z=z, core=core)))
                else:
                    spread.append(w.here(src, dst))
    for copy in twin:
        copy.wait_recv()
    for copy in spread[:2]:
        copy.wait()
    for copy in spread[2:]:
        copy.wait_recv()
    w.finish()


def attend(q, kv, cot, wo, gu_own):
    sds = jax.ShapeDtypeStruct
    return pl.pallas_call(
        attend_kernel,
        out_shape=(
            sds((16, 64, 256), BF),
            sds((2, 64, 2048), BF),
            sds((1024, 256), BF),
            sds((16, 64, 2048), BF),
            sds((8, 2, 128, 2048), BF),
            sds((8, 256, 1536), BF),
        ),
        in_specs=[VMEM] * 5,
        out_specs=[VMEM] * 6,
        scratch_shapes=sems(80, 8),
        compiler_params=pltpu.CompilerParams(
            collective_id=1, has_side_effects=True, vmem_limit_bytes=56 * MB
        ),
        name="attend",
    )(q, kv, cot, wo, gu_own)


def mid_kernel(h2_own, down_own, h2, w_down, send_sem, recv_sem, here_sem):
    p = Place()
    w = Wire(send_sem, recv_sem, here_sem)
    h2[p.t] = h2_own[0]
    h2[15 - p.t] = h2_own[1]
    w_down[p.shard] = down_own[...]
    meet(p.peers(("z", "sib", "x", "cross", "pair")))

    def block(t, k):
        return h2.at[t if k == 0 else 15 - t]

    def part(s, at, n):
        return w_down.at[s, pl.ds(pl.multiple_of(at, 48), n)]

    run(
        gather_z(w, p, lambda k: block(p.t, k), block),
        gather_xy(w, p, lambda at, n: part(p.shard, at, n), part, 96),
    )
    w.finish()


def mid(h2_own, down_own):
    sds = jax.ShapeDtypeStruct
    return pl.pallas_call(
        mid_kernel,
        out_shape=(sds((16, 64, 2048), BF), sds((8, 96, 2048), BF)),
        in_specs=[VMEM] * 2,
        out_specs=[VMEM] * 2,
        scratch_shapes=sems(48, 1),
        compiler_params=pltpu.CompilerParams(
            collective_id=2, has_side_effects=True, vmem_limit_bytes=32 * MB
        ),
        name="mid",
    )(h2_own, down_own)


def add(*vals):
    total = vals[0].astype(F32)
    for val in vals[1:]:
        total = total + val.astype(F32)
    return total


def z_room():
    return [
        pltpu.VMEM((4, 2, 64, 2048), BF),
        pltpu.VMEM((4, 2, 64, 2048), BF),
        pltpu.VMEM((2, 64, 2048), BF),
        pltpu.VMEM((2, 2, 64, 2048), BF),
    ]


def reduce_z(w, p, part, room, out):
    near, mine, relay, last = room
    up, down, sib = p.at(z=p.up(1)), p.at(z=p.up(3)), p.at(core=1 - p.core)

    def block(n, core, k):
        t = 2 * p.up(n) + core
        return t if k == 0 else 15 - t

    first = {}
    for n in (2, 1, 3, 0):
        for k in (0, 1):
            first[n, k] = w.send(part.at[block(n, 1 - p.core, k)], near.at[n, k], sib)

    def fold(n, k):
        first[n, k].wait_recv()
        mine[n, k] = add(part[block(n, p.core, k)], near[n, k]).astype(BF)

    yield
    fold(2, 0)
    e0 = w.send(mine.at[2, 0], relay.at[0], up)
    fold(2, 1)
    e1 = w.send(mine.at[2, 1], relay.at[1], down)
    fold(1, 1)
    a1 = w.send(mine.at[1, 1], last.at[0, 1], up)
    fold(3, 0)
    b0 = w.send(mine.at[3, 0], last.at[1, 0], down)
    fold(1, 0)
    fold(3, 1)
    yield
    fold(0, 0)
    fold(0, 1)
    e0.wait_recv()
    mine[1, 0] = add(mine[1, 0], relay[0]).astype(BF)
    a0 = w.send(mine.at[1, 0], last.at[0, 0], up)
    e1.wait_recv()
    mine[3, 1] = add(mine[3, 1], relay[1]).astype(BF)
    b1 = w.send(mine.at[3, 1], last.at[1, 1], down)
    yield
    for k, (a, b) in enumerate(((a0, b0), (a1, b1))):
        a.wait_recv()
        b.wait_recv()
        out[k] = add(mine[0, k], last[0, k], last[1, k])


def xy_room(rows, cols):
    half = cols // 2
    return [
        pltpu.VMEM((3, 4, rows, half), BF),
        pltpu.VMEM((4, rows, half), BF),
        pltpu.VMEM((3, rows, half), BF),
    ] * 2


def reduce_xy(w, p, part, room, out):
    ra, sa, fa, rb, sb, fb = room
    half = part.shape[3] // 2
    left, right = pl.ds(0, half), pl.ds(half, half)
    spans = (1, 2, 3)
    easts = [p.at(x=p.east(d)) for d in spans]
    norths = [p.north(d) for d in spans]
    ca = [w.send(part.at[p.east(d), :, :, left], ra.at[d - 1], easts[d - 1]) for d in spans]
    cb = [
        w.send(part.at[:, lax.rem(p.y + d, 4), :, right], rb.at[d - 1], norths[d - 1])
        for d in spans
    ]
    yield
    yield
    for copy in ca:
        copy.wait_recv()

    @pl.loop(0, 4)
    def _(y):
        sa[y] = add(part[p.x, y, :, left], ra[0, y], ra[1, y], ra[2, y]).astype(BF)

    da = [w.send(sa.at[lax.rem(p.y + d, 4)], fa.at[d - 1], norths[d - 1]) for d in spans]
    yield
    for copy in cb:
        copy.wait_recv()

    @pl.loop(0, 4)
    def _(x):
        sb[x] = add(part[x, p.y, :, right], rb[0, x], rb[1, x], rb[2, x]).astype(BF)

    db = [w.send(sb.at[p.east(d)], fb.at[d - 1], easts[d - 1]) for d in spans]
    yield
    for copy in da:
        copy.wait_recv()
    out[:, left] = add(sa[p.y], fa[0], fa[1], fa[2]).astype(BF)
    yield
    for copy in db:
        copy.wait_recv()
    out[:, right] = add(sb[p.x], fb[0], fb[1], fb[2]).astype(BF)


def sums_kernel(part, grads, out, mine, *rest):
    zr, xr, (send_sem, recv_sem, here_sem) = rest[:4], rest[4:10], rest[10:]
    p = Place()
    w = Wire(send_sem, recv_sem, here_sem)
    meet(p.peers(("z", "sib", "plane")))
    run(reduce_z(w, p, part, zr, out), reduce_xy(w, p, grads, xr, mine))
    w.finish()


def sums(part, grads, cid):
    sds = jax.ShapeDtypeStruct
    _, _, rows, cols = grads.shape
    return pl.pallas_call(
        sums_kernel,
        out_shape=(sds((2, 64, 2048), F32), sds((rows, cols), BF)),
        in_specs=[VMEM] * 2,
        out_specs=[VMEM] * 2,
        scratch_shapes=z_room() + xy_room(rows, cols) + sems(32, 1),
        compiler_params=pltpu.CompilerParams(
            collective_id=cid, has_side_effects=True, vmem_limit_bytes=40 * MB
        ),
        name="sums",
    )(part, grads)


def sums2_kernel(part, grads, more, out, mine, mine2, *rest):
    zr, xr, yr, (send_sem, recv_sem, here_sem) = rest[:4], rest[4:10], rest[10:16], rest[16:]
    p = Place()
    w = Wire(send_sem, recv_sem, here_sem)
    meet(p.peers(("z", "sib", "plane")))
    run(
        reduce_z(w, p, part, zr, out),
        reduce_xy(w, p, grads, xr, mine),
        reduce_xy(w, p, more, yr, mine2),
    )
    w.finish()


def sums2(part, grads, more, cid):
    sds = jax.ShapeDtypeStruct
    (_, _, r1, c1), (_, _, r2, c2) = grads.shape, more.shape
    return pl.pallas_call(
        sums2_kernel,
        out_shape=(sds((2, 64, 2048), F32), sds((r1, c1), BF), sds((r2, c2), BF)),
        in_specs=[VMEM] * 3,
        out_specs=[VMEM] * 3,
        scratch_shapes=z_room() + xy_room(r1, c1) + xy_room(r2, c2) + sems(48, 1),
        compiler_params=pltpu.CompilerParams(
            collective_id=cid, has_side_effects=True, vmem_limit_bytes=40 * MB
        ),
        name="sums2",
    )(part, grads, more)


def attend_back_kernel(
    q, kv, kv_far, d_tok, dz_own, mixed_part, gu_part, dq, dkv, dz, mixed, gu_mine,
    do, acc, acc_far, out_far, in_far, *rest
):
    zr, xr, (send_sem, recv_sem, here_sem) = rest[:4], rest[4:10], rest[10:]
    p = Place()
    w = Wire(send_sem, recv_sem, here_sem)
    dz[p.t] = dz_own[0]
    dz[15 - p.t] = dz_own[1]
    meet(p.peers(("tp", "plane")))
    pair = p.at(yl=1 - p.yl)
    spread = []
    for dz_ in (2, 1, 3, 0):
        for dc in (0, 1):
            z, core = p.up(dz_), lax.rem(p.core + dc, 2)
            cols = pl.ds(pl.multiple_of((2 * z + core) * 256, 256), 256)
            for k in (0, 1):
                if dz_ or dc:
                    dst = do.at[p.t if k == 0 else 15 - p.t]
                    spread.append(w.send(d_tok.at[k, :, cols], dst, p.at(z=z, core=core)))
                else:
                    do[p.t if k == 0 else 15 - p.t] = d_tok[k, :, cols]

    def block(t, k):
        return dz.at[t if k == 0 else 15 - t]

    tasks = [
        reduce_xy(w, p, gu_part, xr, gu_mine),
        gather_z(w, p, lambda k: block(p.t, k), block),
        reduce_z(w, p, mixed_part, zr, mixed),
    ]
    advance(tasks)
    acc[...] = jnp.zeros_like(acc)
    acc_far[...] = jnp.zeros_like(acc_far)
    for copy in spread:
        copy.wait_recv()
    back = []
    for j in range(7, -1, -1):
        at = pl.ds(j * 128, 128)
        keys = pl.ds(0, j * 128 + 128)
        tri, seen = edges(p, j)
        qj = both(q, at)
        dj = jnp.concatenate(
            [do[2 * j : 2 * j + 2, :, n * 128 : n * 128 + 128].reshape(128, 128) for n in (0, 1)], 0
        )
        near = weights_of(qj, kv[keys, 0:128], j, tri)
        far = weights_of(qj, kv_far[keys, 0:128], j, seen)
        scale = 1.0 / (jnp.sum(near, -1, keepdims=True) + jnp.sum(far, -1, keepdims=True))
        near = near * scale
        far = far * scale
        d_near = dot_t(dj, kv[keys, 128:256])
        d_far = dot_t(dj, kv_far[keys, 128:256])
        delta = jnp.sum(near * d_near, -1, keepdims=True) + jnp.sum(
            far * d_far, -1, keepdims=True
        )
        s_near = (near * (d_near - delta)).astype(BF)
        s_far = (far * (d_far - delta)).astype(BF)
        grad = jnp.dot(s_near, kv[keys, 0:128], preferred_element_type=F32)
        grad += jnp.dot(s_far, kv_far[keys, 0:128], preferred_element_type=F32)
        grad = (grad * 128**-0.5).astype(BF)
        dq[at, 0:128] = grad[:128]
        dq[at, 128:256] = grad[128:]
        acc[keys, 0:128] += t_dot(s_near, qj)
        acc_far[keys, 0:128] += t_dot(s_far, qj)
        acc[keys, 128:256] += t_dot(near.astype(BF), dj)
        acc_far[keys, 128:256] += t_dot(far.astype(BF), dj)
        out_far[at, 0:128] = (acc_far[at, 0:128] * 128**-0.5).astype(BF)
        out_far[at, 128:256] = acc_far[at, 128:256].astype(BF)
        back.append((at, w.send(out_far.at[at], in_far.at[at], pair)))
        advance(tasks)
    run(*tasks)
    for at, copy in back:
        copy.wait_recv()
        dkv[at, 0:128] = add(acc[at, 0:128] * 128**-0.5, in_far[at, 0:128]).astype(BF)
        dkv[at, 128:256] = add(acc[at, 128:256], in_far[at, 128:256]).astype(BF)
    w.finish()


def attend_back(q, kv, kv_far, d_tok, dz_own, mixed_part, gu_part):
    sds = jax.ShapeDtypeStruct
    return pl.pallas_call(
        attend_back_kernel,
        out_shape=(
            sds((1024, 256), BF),
            sds((1024, 256), BF),
            sds((16, 64, 2048), BF),
            sds((2, 64, 2048), F32),
            sds((128, 1536), BF),
        ),
        in_specs=[VMEM] * 7,
        out_specs=[VMEM] * 5,
        scratch_shapes=[
            pltpu.VMEM((16, 64, 256), BF),
            pltpu.VMEM((1024, 256), F32),
            pltpu.VMEM((1024, 256), F32),
            pltpu.VMEM((1024, 256), BF),
            pltpu.VMEM((1024, 256), BF),
        ]
        + z_room()
        + xy_room(128, 1536)
        + sems(80, 1),
        compiler_params=pltpu.CompilerParams(
            collective_id=4, has_side_effects=True, vmem_limit_bytes=58 * MB
        ),
        name="attend_back",
    )(q, kv, kv_far, d_tok, dz_own, mixed_part, gu_part)


def last_kernel(cols, rows, vec, cols_out, rows_out, vec_out, ra, rb, rc, send_sem, recv_sem, here_sem):
    p = Place()
    w = Wire(send_sem, recv_sem, here_sem)
    meet(p.peers(("tp", "plane", "swap")))
    stay = p.yl == p.core
    cols_out[p.t] = cols[p.t]
    ra[p.t] = vec[...]
    moves = []
    for dz in range(4):
        for dc in range(2):
            if dz or dc:
                z, core = p.up(dz), lax.rem(p.core + dc, 2)
                peer = p.at(z=z, core=core)
                moves.append(w.send(vec, ra.at[p.t], peer))
                moves.append(w.send(cols.at[2 * z + core], cols_out.at[p.t], peer))
    n = w.n
    swap = pltpu.make_async_remote_copy(
        src_ref=rows,
        dst_ref=rows_out,
        send_sem=send_sem.at[n],
        recv_sem=recv_sem.at[n],
        device_id=p.at(yl=1 - p.yl, core=1 - p.core),
        device_id_type=MESH,
    )
    w.n += 1

    @pl.when(jnp.logical_not(stay))
    def _():
        swap.start()

    @pl.when(stay)
    def _():
        rows_out[...] = rows[...]

    for copy in moves[0::2]:
        copy.wait_recv()
    rb[p.x] = sum((ra[i] for i in range(1, 8)), ra[0])
    xs = [w.send(rb.at[p.x], rb.at[p.x], p.at(x=p.east(d))) for d in (1, 2, 3)]
    for copy in xs:
        copy.wait_recv()
    rc[p.y] = sum((rb[i] for i in range(1, 4)), rb[0])
    ys = [w.send(rc.at[p.y], rc.at[p.y], p.north(d)) for d in (1, 2, 3)]
    for copy in ys:
        copy.wait_recv()
    vec_out[...] = sum((rc[i] for i in range(1, 4)), rc[0])
    for copy in moves[1::2]:
        copy.wait_recv()

    @pl.when(jnp.logical_not(stay))
    def _():
        swap.wait()

    w.finish()


def last(cols, rows, vec):
    sds = jax.ShapeDtypeStruct
    n = vec.shape
    return pl.pallas_call(
        last_kernel,
        out_shape=(sds(cols.shape, BF), sds(rows.shape, BF), sds(n, F32)),
        in_specs=[VMEM] * 3,
        out_specs=[VMEM] * 3,
        scratch_shapes=[
            pltpu.VMEM((8,) + n, F32),
            pltpu.VMEM((4,) + n, F32),
            pltpu.VMEM((4,) + n, F32),
        ]
        + sems(32, 1),
        compiler_params=pltpu.CompilerParams(
            collective_id=6, has_side_effects=True, vmem_limit_bytes=32 * MB
        ),
        name="last",
    )(cols, rows, vec)


def rotary(positions, width):
    half = width // 2
    freq = THETA ** (-2.0 * jnp.arange(half, dtype=F32) / width)
    angle = positions.astype(F32)[:, None] * freq[None, :]
    cosine = jnp.concatenate([jnp.cos(angle), jnp.cos(angle)], 1)
    sine = jnp.concatenate([-jnp.sin(angle), jnp.sin(angle)], 1)
    return (cosine, sine)


def turn_back(grads, cosine, sine):
    moved = grads * sine
    half = grads.shape[-1] // 2
    return grads * cosine + jnp.concatenate([moved[..., half:], moved[..., :half]], -1)


def row_norm(vals):
    scale = lax.rsqrt(jnp.mean(vals * vals, -1, keepdims=True) + EPS)
    return (vals * scale, scale)


def norm_back(grad_unit, unit, scale):
    return scale * (grad_unit - unit * jnp.mean(grad_unit * unit, -1, keepdims=True))


def mm(left, right):
    return jnp.dot(left, right, preferred_element_type=F32)


def mm_t(left, right):
    return lax.dot_general(left, right, (((1,), (1,)), ((), ())), preferred_element_type=F32)


def t_mm(left, right):
    return lax.dot_general(left, right, (((0,), (0,)), ((), ())), preferred_element_type=F32)


def gather(val, axes):
    return lax.all_gather(val, axes, axis=0, tiled=True)


def scatter(val, axes):
    return lax.psum_scatter(val, axes, scatter_dimension=0, tiled=True)


def to_sorted(val):
    a = val.reshape(8, 2, 64, -1)
    return jnp.concatenate([a[:, 0], a[::-1, 1]], 0).reshape(1024, -1)


def to_owner(val):
    a = val.reshape(16, 64, -1)
    return jnp.stack([a[:8], a[:7:-1]], 1).reshape(1024, -1)


def gather_tp(val):
    return to_sorted(gather(val, TP))


def scatter_tp(val):
    return scatter(to_owner(val.astype(BF)), TP).astype(F32)


def shards(
    tokens,
    gain_in,
    query_weight,
    key_weight,
    value_weight,
    gain_query,
    gain_key,
    out_weight,
    gain_mid,
    gate_weight,
    up_weight,
    down_weight,
    cotangent,
):
    width = tokens.shape[4]
    n_z, n_yl, n_core = (lax.axis_size(a) for a in ("z", "yl", "core"))
    n_tp = n_z * n_core
    n_fs = lax.axis_size("x") * lax.axis_size("yh")
    rows = 128
    head = 128
    qc, kc, fc = 256, 128, 768
    factor = head ** (-0.5)
    t = lax.axis_index(TP)
    yl = lax.axis_index("yl")

    def positions(lane):
        idx = jnp.arange(1024, dtype=jnp.int32)
        tile, spot = idx // 128, idx % 128
        place = jnp.where(tile < 4, 2 * tile + lane, 2 * tile + 1 - lane)
        return place * 128 + spot

    query_pos = positions(yl)
    key_pos = jnp.concatenate([query_pos, positions(1 - yl)])
    allowed = key_pos[None, :] <= query_pos[:, None]
    cosine, sine = rotary(query_pos, head)

    cut = lambda w, n: lax.dynamic_slice_in_dim(w, t * n, n, 1)
    gu_own = jnp.concatenate([cut(gate_weight, fc), cut(up_weight, fc)], 1)
    d_s = down_weight.shape[0] // n_tp
    rows_d = lax.ppermute(
        lax.dynamic_slice_in_dim(down_weight, t * d_s, d_s, 0),
        TP + FS,
        [(a * n_fs + b, b * n_fs + a) for a in range(n_tp) for b in range(n_fs)],
    )

    tok = tokens.reshape(2, 64, width)
    x = tokens.reshape(rows, width).astype(F32)
    unit_in, scale_in = row_norm(x)
    grad_l = cotangent.reshape(rows, width)
    h, w_qkv, query_b, kv, raw = front(
        tok,
        gain_in.reshape(1, -1),
        jnp.concatenate([cut(query_weight, qc), cut(key_weight, kc), cut(value_weight, kc)], 1),
        cosine,
        sine,
        gain_query.reshape(1, -1),
        gain_key.reshape(1, -1),
    )
    h = h.reshape(1024, width)
    attended, o_tok, kv_far, g, w_out, w_gu = attend(query_b, kv, cotangent.reshape(2, 64, width),
        lax.dynamic_slice_in_dim(out_weight, lax.axis_index("core") * 128, 128, 0),
        gu_own,
    )
    w_gu = w_gu.reshape(2048, 2 * fc)
    attended = attended.reshape(1024, qc)
    g = g.reshape(1024, width)
    w_out = w_out.reshape(2048, 2048)
    unit_q, scale_q = row_norm(raw[:, :qc].reshape(-1, 2, head))
    unit_k, scale_k = row_norm(raw[:, qc : qc + kc].reshape(-1, 1, head))
    y_mid = x + mm(o_tok.reshape(rows, width), w_out)
    unit_mid, scale_mid = row_norm(y_mid)
    h2, w_down = mid((unit_mid * gain_mid).astype(BF).reshape(2, 64, width), rows_d)
    h2, w_down = h2.reshape(1024, width), w_down.reshape(768, width)
    gu = mm(h2, w_gu)
    gate, upper = gu[:, :fc], gu[:, fc:]
    sig = jax.nn.sigmoid(gate)
    silu_gate = gate * sig
    act_b = (silu_gate * upper).astype(BF)
    mixed_part = mm(act_b, w_down).astype(BF).reshape(16, 64, width)
    grad_act = mm_t(g, w_down)
    dgate_b = (grad_act * upper * sig * (1.0 + gate * (1.0 - sig))).astype(BF)
    dup_b = (grad_act * silu_gate).astype(BF)
    dgu = jnp.concatenate([dgate_b, dup_b], 1)

    def rows_to_owners(part):
        cols = part.shape[1]
        part = part.astype(BF).reshape(2, 4, 2, -1, cols)
        return part.transpose(1, 2, 0, 3, 4).reshape(4, 4, -1, cols)

    def cols_to_owners(part):
        cols = part.shape[1]
        part = part.astype(BF).reshape(n_z, n_yl, n_core, 4, 2, 16, cols)
        return part.transpose(3, 4, 1, 0, 2, 5, 6).reshape(4, 4, 128, cols)

    grad_h2, down_mine = sums(
        mm_t(dgu, w_gu).astype(BF).reshape(16, 64, width), rows_to_owners(t_mm(act_b, g)), 3
    )
    grad_h2 = grad_h2.reshape(rows, width)
    term_mid = jnp.sum(grad_h2 * unit_mid, 0)
    grad_mid = grad_l.astype(F32) + norm_back(grad_h2 * gain_mid, unit_mid, scale_mid)
    dz_own = grad_mid.astype(BF)
    d_tok = mm_t(dz_own, w_out).astype(BF)
    grad_query, own, dz, mlp_out, gu_mine = attend_back(
        query_b,
        kv,
        kv_far,
        d_tok.reshape(2, 64, width),
        dz_own.reshape(2, 64, width),
        mixed_part,
        cols_to_owners(t_mm(h2, dgu)),
    )
    dz = dz.reshape(1024, width)
    mixed = (y_mid + mlp_out.reshape(rows, width)).astype(BF)
    dv_b = own[:, head:]
    cos3, sin3 = cosine[:, None, :], sine[:, None, :]
    grad_q_norm = turn_back(grad_query.astype(F32).reshape(-1, 2, head), cos3, sin3)
    grad_k_norm = turn_back(own[:, :head].astype(F32).reshape(-1, 1, head), cos3, sin3)
    term_query = jnp.sum(grad_q_norm * unit_q, (0, 1))
    term_key = jnp.sum(grad_k_norm * unit_k, (0, 1))
    dq_b = norm_back(grad_q_norm * gain_query, unit_q, scale_q).reshape(-1, qc).astype(BF)
    dk_b = norm_back(grad_k_norm * gain_key, unit_k, scale_k).reshape(-1, kc).astype(BF)
    dqkv = jnp.concatenate([dq_b, dk_b, dv_b], 1)
    grad_h, qkv_mine, out_mine = sums2(
        mm_t(dqkv, w_qkv).astype(BF).reshape(16, 64, width),
        cols_to_owners(t_mm(h, dqkv)),
        rows_to_owners(t_mm(attended, dz)),
        5,
    )
    grad_h = grad_h.reshape(rows, width)
    term_in = jnp.sum(grad_h * unit_in, 0)
    tokens_grad = (grad_mid + norm_back(grad_h * gain_in, unit_in, scale_in)).astype(BF)

    mine = jnp.concatenate([gu_mine, qkv_mine], 1).reshape(n_tp, 16, -1)
    late = jnp.concatenate([down_mine, out_mine], 0)
    terms = jnp.concatenate([term_in, term_mid, term_query, term_key, jnp.zeros((768,), F32)])
    mine, late, terms = last(mine, late, terms.reshape(40, 128))
    mine = mine.transpose(1, 0, 2).astype(F32)

    def take(at, n):
        return mine[:, :, at : at + n].reshape(-1, n_tp * n)

    grad_gate_w, grad_up_w = take(0, fc), take(fc, fc)
    grad_q_w, grad_k_w, grad_v_w = (
        take(2 * fc, qc),
        take(2 * fc + qc, kc),
        take(2 * fc + qc + kc, kc),
    )
    late = late.astype(F32)
    grad_down, grad_out = late[:48], late[48:]
    terms = terms.reshape(-1)
    sum_in, sum_mid = terms[:width], terms[width : 2 * width]
    sum_query, sum_key = terms[2 * width : 2 * width + head], terms[2 * width + head : 2 * width + 2 * head]
    return (
        mixed.reshape(tokens.shape),
        tokens_grad.reshape(tokens.shape),
        sum_in,
        grad_q_w,
        grad_k_w,
        grad_v_w,
        sum_query,
        sum_key,
        grad_out,
        sum_mid,
        grad_gate_w,
        grad_up_w,
        grad_down,
    )


def solution(mesh):
    fine = Mesh(mesh.devices.reshape(4, 2, 2, 4, 2), ALL)
    ctx, fsdp = ("z", "yl", "core"), FS
    act = P(fsdp, None, ctx, None, None)
    weight = P(fsdp, None)
    grad = P(ctx + fsdp, None)
    placed = (
        act, P(), weight, weight, weight, P(), P(), weight, P(), weight, weight, weight, act,
    )
    return jax.shard_map(
        shards,
        mesh=fine,
        in_specs=placed,
        out_specs=(act, act, P(), grad, grad, grad, P(), P(), grad, P(), grad, grad, grad),
        check_vma=False,
    )
```

time: 1010 us -> 476 us (0.47)
  waiting for transfers between devices: 652 us -> 0.01 us
  Pallas kernels: 14.6 us -> 348 us
  blocking collectives: 95.7 us -> 0 us
  matrix products: 118 us -> 55.4 us
  other arithmetic: 49.2 us -> 22.5 us
  between operations: 15.3 us -> 1.86 us
    reduce_scatter x8 -> x0, waiting for transfers between devices: 356 us -> none  [scatter(): return lax.psum_scatter(val, axes, scatter_dimension=0, tiled=True)]
    pallas_call x1 -> x7, Pallas kernels: 14.6 us -> 348 us  [the longest x1 113 us: attend(): pl.pallas_call(attend_kernel, out_shape=(sds((16, 64, 256), BF), sds((2,...]
    all_gather x7 -> x0, waiting for transfers between devices: 262 us -> none  [gather(): return lax.all_gather(val, axes, axis=0, tiled=True)]
    psum x1 -> x0, blocking collectives: 68.6 us -> none  [shards(): lax.psum((term_in, term_mid, term_query, term_key), ALL)]
    ppermute x2 -> x1, waiting for transfers between devices: 32.9 us -> 0.01 us  [shards(): lax.ppermute(lax.dynamic_slice_in_dim(down_weight, t * d_s, d_s, 0), TP +...]
    dot_general x5 -> x0, matrix products: 30.5 us -> none  [the longest x1 8.27 us: shards(): jnp.einsum('jts,tjd->sd', probs_b, do_b, preferred_element_type=F32)]
    all_to_all x1 -> x0, blocking collectives: 27.2 us -> none  [shards(): lax.all_to_all(mine, TP, 0, 0, tiled=True).transpose(1, 0, 2).astype(F32)]
    convert_element_type x7 -> x3, other arithmetic: 15.9 us -> 0.58 us  [the longest x1 0.33 us: shards(): dz_own = grad_mid.astype(BF)]
  transfers between devices with their start and end apart: 17 -> 1, of which waited for: 15 -> 0; matrix products, arithmetic and copies ran while one was open for 13% -> 5% of each run, Pallas kernels for 1% -> 34%
where the time goes in v3:
time: 476 us; the launch traced here: 473 us
  Pallas kernels  348 us (73%)
  matrix products  55.4 us (12%)
  local copies, waits for them, and re-layouts  39 us (8%)
  other arithmetic  22.5 us (5%)
  starting transfers between devices  6.2 us (1%)
    pallas_call x1, Pallas kernels, attend(): pl.pallas_call(attend_kernel, out_shape=(sds((16, 64, 256), BF), sds((2,...  113 us
    pallas_call x1, Pallas kernels, attend_back(): pl.pallas_call(attend_back_kernel, out_shape=(sds((1024, 256), BF), sds((...  66.7 us
    pallas_call x1, Pallas kernels, front(): pl.pallas_call(front_kernel, out_shape=(sds((16, 64, 2048), BF), sds((204...  47.5 us
    pallas_call x1, Pallas kernels, mid(): pl.pallas_call(mid_kernel, out_shape=(sds((16, 64, 2048), BF), sds((8, 96...  39.6 us
    pallas_call x1, Pallas kernels, sums2(): pl.pallas_call(sums2_kernel, out_shape=(sds((2, 64, 2048), F32), sds((r1,...  31.9 us
    pallas_call x1, Pallas kernels, sums(): pl.pallas_call(sums_kernel, out_shape=(sds((2, 64, 2048), F32), sds((rows...  30 us
    dot_general x3, matrix products, mm(): return jnp.dot(left, right, preferred_element_type=F32)  19.9 us
    dot_general x4, matrix products, mm_t(): lax.dot_general(left, right, (((1,), (1,)), ((), ())), preferred_element_...  18.6 us
  transfers between devices with their start and end apart: 1, of which 0 were waited for; matrix products, arithmetic and copies ran while one was open for 5% of the time, Pallas kernels for 34%

profile of v3, /device:TPU:1, one launch (start us, length us, event | category | flops | bytes accessed | tf_op | source)
XLA Modules:
  0.0 472.6 jit_solution(12871365433687768069)
XLA Ops:
  3.3 6.2 %collective-permute-start = (bf16[96,2048]{1,0:T(8,128)(2,1)}, bf16[96,2048]{1,0:T(8,128)(2,1)S(1)}, u32[]{:S(2)}, u32[]{:S(2)}) collective-permute-start(bf16[96,2048]{1,0:T(8,128)(2,1)} %constant_dynamic-slice_fusion), channel_id=1, source_target_pairs={{0,0},{1,8},{2,32},{3,40},{4,64},{5,72},{6,96},{7,104},{8,1},{9,9}... | collective-permute-start | bytes 1179656 | tf_op jit(solution)/shard_map/ppermute | solution.py:894
  14.0 47.5 %front.1 = (bf16[16,64,2048]{2,1,0:T(8,128)(2,1)}, bf16[2048,512]{1,0:T(8,128)(2,1)}, bf16[1024,256]{1,0:T(8,128)(2,1)S(1)}, bf16[1024,256]{1,0:T(8,128)(2,1)S(1)}, f32[1024,384]{1,0:T(8,128)S(1)}) custom-call(bf16[2,64,2048]{2,1,0:T(8,128)(2,1)S(1)} %bitcast.179, f32[1,2048]{1,0:T(1,128)S(1)} %bitcast.188, bf16[256,512]{1,0:T(8,128)(2,1)S(1)} %pad_maximum_fusion.11.w_own, ...), custom_call_target="tpu_custom_call" | custom-call | tf_op jit(solution)/shard_map/front/pallas_call | solution.py:263
  70.5 113.4 %attend.1 = (bf16[16,64,256]{2,1,0:T(8,128)(2,1)}, bf16[2,64,2048]{2,1,0:T(8,128)(2,1)}, bf16[1024,256]{1,0:T(8,128)(2,1)}, bf16[16,64,2048]{2,1,0:T(8,128)(2,1)...) custom-call(bf16[1024,256]{1,0:T(8,128)(2,1)} %copy-done.13, bf16[1024,256]{1,0:T(8,128)(2,1)} %copy-done.14, ...), custom_call_target="tpu_custom_call" | custom-call | tf_op jit(solution)/shard_map/attend/pallas_call | solution.py:388
  184.0 5.0 %multiply_reduce_fusion.7 = (f32[128]{0:T(128)S(1)}, f32[128,2048]{1,0:T(8,128)S(1)}) fusion(bf16[128,2048]{1,0:T(8,128)(2,1)} %bitcast.212, bf16[2048,2048]{1,0:T(8,128)(2,1)} %bitcast.196, bf16[128,2048]{1,0:T(8,128)(2,1)S(1)} %bitcast.180), kind=kOutput, calls=%fused_computation.48 | convolution fusion | flops 1074790272 | bytes 10486272 | tf_op jit(solution)/shard_map/dot_general | solution.py:817
  194.3 39.6 %mid.1 = (bf16[16,64,2048]{2,1,0:T(8,128)(2,1)S(1)}, bf16[8,96,2048]{2,1,0:T(8,128)(2,1)S(1)}) custom-call(bf16[2,64,2048]{2,1,0:T(8,128)(2,1)S(1)} %bitcast.186, bf16[96,2048]{1,0:T(8,128)(2,1)S(1)} %collective-permute-done.down_own), custom_call_target="tpu_custom_call" | custom-call | tf_op jit(solution)/shard_map/mid/pallas_call | solution.py:431
  233.9 9.8 %fusion.38 = f32[1024,1536]{0,1:T(8,128)S(1)} fusion(bf16[1024,2048]{1,0:T(8,128)(2,1)S(1)} %bitcast.192, bf16[2048,1536]{1,0:T(8,128)(2,1)} %bitcast.221), kind=kOutput, calls=%fused_computation.130 | convolution fusion | flops 6442450944 | bytes 16777216 | tf_op jit(solution)/shard_map/dot_general | solution.py:817
  243.7 5.6 %multiply_convert_fusion.2 = (bf16[1024,768]{0,1:T(8,128)(2,1)S(1)}, bf16[1024,768]{0,1:T(8,128)(2,1)}, bf16[1024,768]{0,1:T(8,128)(2,1)S(1)}) fusion(f32[1024,1536]{0,1:T(8,128)S(1)} %fusion.38, bf16[1024,2048]{1,0:T(8,128)(2,1)S(1)} %bitcast.226, bf16[768,2048]{1,0:T(8,128)(2,1)S(1)} %bitcast.194), kind=kOutput, calls=%fused_computation.8 | convolution fusion | flops 3233021952 | bytes 18350080 | tf_op jit(solution)/shard_map/dot_general | solution.py:821
  249.3 3.6 convolution_convert_fusion.4
  253.0 5.1 %convolution_convert_fusion.3 = bf16[1024,2048]{1,0:T(8,128)(2,1)} fusion(bf16[1024,768]{0,1:T(8,128)(2,1)S(1)} %get-tuple-element.115, bf16[768,2048]{1,0:T(8,128)(2,1)S(1)} %bitcast.195), kind=kOutput, calls=%fused_computation.3 | convolution fusion | flops 3223322624 | bytes 8912896 | tf_op jit(solution)/shard_map/dot_general | solution.py:817
  258.1 7.0 %convolution_convert_fusion.1 = bf16[1024,2048]{1,0:T(8,128)(2,1)S(1)} fusion(bf16[2048,1536]{1,0:T(8,128)(2,1)S(1)} %bitcast.224, bf16[1024,768]{0,1:T(8,128)(2,1)S(1)} %copy-done.50, bf16[1024,768]{0,1:T(8,128)(2,1)S(1)} %get-tuple-element.113), kind=kOutput, calls=%fused_computation.1 | convolution fusion | flops 6450839552 | bytes 13631488 | tf_op jit(solution)/shard_map/dot_general | solution.py:821
  265.1 9.6 %convolution_convert_fusion = bf16[2048,1536]{1,0:T(8,128)(2,1)} fusion(bf16[1024,2048]{1,0:T(8,128)(2,1)S(1)} %bitcast.193, bf16[1024,768]{0,1:T(8,128)(2,1)S(1)} %copy-done.50, bf16[1024,768]{0,1:T(8,128)(2,1)S(1)} %get-tuple-element.113), kind=kOutput, calls=%fused_computation | convolution fusion | flops 6451888128 | bytes 13631488 | tf_op jit(solution)/shard_map/dot_general | solution.py:825
  275.1 30.0 %sums.1 = (f32[2,64,2048]{2,1,0:T(8,128)S(1)}, bf16[48,2048]{1,0:T(8,128)(2,1)S(1)}) custom-call(bf16[16,64,2048]{2,1,0:T(8,128)(2,1)S(1)} %bitcast.184, bf16[4,4,48,2048]{3,2,1,0:T(8,128)(2,1)S(1)} %bitcast.181), custom_call_target="tpu_custom_call" | custom-call | tf_op jit(solution)/shard_map/sums/pallas_call | solution.py:566
  305.9 3.7 convolution_convert_fusion.6
  309.6 6.1 %copy.50 = bf16[4,2,2,4,2,16,1536]{6,5,2,0,1,4,3:T(8,128)(2,1)} copy(bf16[4,2,2,4,2,16,1536]{6,5,4,3,2,1,0:T(8,128)(2,1)} %bitcast.201) | data formatting | bytes 12582912 | tf_op jit(solution)/shard_map/reshape | solution.py:946
  315.7 66.7 %attend_back.1 = (bf16[1024,256]{1,0:T(8,128)(2,1)}, bf16[1024,256]{1,0:T(8,128)(2,1)}, bf16[16,64,2048]{2,1,0:T(8,128)(2,1)}, f32[2,64,2048]{2,1,0:T(8,128)}, bf16[128,1536]{1,0:T(8,128)(2,1)}) custom-call(bf16[1024,256]{1,0:T(8,128)(2,1)} %copy-done.13, bf16[1024,256]{1,0:T(8,128)(2,1)} %copy-done.14, bf16[1024,256]{1,0:T(8,128)(2,1)} %get-tuple-element.43.kv_far, ...), custom_call_target="tpu_custom_call" | custom-call | tf_op jit(solution)/shard_map/attend_back/pallas_call | solution.py:688
  386.8 2.5 reshape.345
  389.3 1.9 broadcast_multiply_fusion
  392.5 4.2 multiply_reduce_fusion.3
  401.9 2.4 convolution_convert_fusion.2
  404.3 2.5 convolution_convert_fusion.5
  407.0 1.9 copy-done.46
  410.3 31.9 %sums2.1 = (f32[2,64,2048]{2,1,0:T(8,128)S(1)}, bf16[128,512]{1,0:T(8,128)(2,1)S(1)}, bf16[16,2048]{1,0:T(8,128)(2,1)S(1)}) custom-call(bf16[16,64,2048]{2,1,0:T(8,128)(2,1)S(1)} %bitcast.183, bf16[4,4,128,512]{3,2,1,0:T(8,128)(2,1)S(1)} %bitcast.182, bf16[4,4,16,2048]{3,2,1,0:T(8,128)(2,1)S(1)} %bitcast.185), custom_call_target="tpu_custom_call" | custom-call | tf_op jit(solution)/shard_map/sums2/pallas_call | solution.py:595
  442.8 18.5 %last.1 = (bf16[8,16,2048]{2,1,0:T(8,128)(2,1)S(1)}, bf16[64,2048]{1,0:T(8,128)(2,1)S(1)}, f32[40,128]{1,0:T(8,128)S(1)}) custom-call(bf16[8,16,2048]{2,1,0:T(8,128)(2,1)S(1)} %bitcast.187, bf16[64,2048]{1,0:T(8,128)(2,1)S(1)} %pad_maximum_fusion.12.rows, f32[40,128]{1,0:T(8,128)S(1)} %bitcast.189), custom_call_target="tpu_custom_call" | custom-call | tf_op jit(solution)/shard_map/last/pallas_call | solution.py:774
  468.3 4.1 fusion.8
  (178 shorter events, 41.9 us)
Async XLA Ops:
  0.7 13.3 %copy-start.15 = (f32[2048]{0:T(1024)S(1)}, f32[2048]{0:T(1024)}, u32[]{:S(2)}) copy-start(f32[2048]{0:T(1024)} %param.14) | copy-start | bytes 24580
  0.7 13.3 %copy-start.17 = (f32[128]{0:T(128)S(1)}, f32[128]{0:T(128)}, u32[]{:S(2)}) copy-start(f32[128]{0:T(128)} %param.18) | copy-start | bytes 1540
  0.7 13.3 %copy-start.16 = (f32[128]{0:T(128)S(1)}, f32[128]{0:T(128)}, u32[]{:S(2)}) copy-start(f32[128]{0:T(128)} %param.19) | copy-start | bytes 1540
  3.3 190.9 %collective-permute-start = (bf16[96,2048]{1,0:T(8,128)(2,1)}, bf16[96,2048]{1,0:T(8,128)(2,1)S(1)}, u32[]{:S(2)}, u32[]{:S(2)}) collective-permute-start(bf16[96,2048]{1,0:T(8,128)(2,1)} %constant_dynamic-slice_fusion), channel_id=1, source_target_pairs={{0,0},{1,8},{2,32},{3,40},{4,64},{5,72},{6,96},{7,104},{8,1},{9,9}... | collective-permute-start | bytes 1179656 | tf_op jit(solution)/shard_map/ppermute | solution.py:894
  13.9 55.6 %copy-start.8 = (f32[1024,128]{1,0:T(8,128)}, f32[1024,128]{1,0:T(8,128)S(1)}, u32[]{:S(2)}) copy-start(f32[1024,128]{1,0:T(8,128)S(1)} %get-tuple-element.140.sine) | copy-start | bytes 1572868
  13.9 55.6 %copy-start.10 = (f32[1024,128]{1,0:T(8,128)}, f32[1024,128]{1,0:T(8,128)S(1)}, u32[]{:S(2)}) copy-start(f32[1024,128]{1,0:T(8,128)S(1)} %get-tuple-element.139.cosine) | copy-start | bytes 1572868
  63.0 7.5 %copy-start.6 = (f32[1024,384]{1,0:T(8,128)}, f32[1024,384]{1,0:T(8,128)S(1)}, u32[]{:S(2)}) copy-start(f32[1024,384]{1,0:T(8,128)S(1)} %get-tuple-element.50) | copy-start | bytes 4718596
  68.3 115.7 %copy-start.3 = (bf16[1,2,1,64,2048]{4,3,2,1,0:T(8,128)(2,1)S(1)}, bf16[1,2,1,64,2048]{4,3,2,1,0:T(8,128)(2,1)}, u32[]{:S(2)}) copy-start(bf16[1,2,1,64,2048]{4,3,2,1,0:T(8,128)(2,1)} %param.13) | copy-start | bytes 1572868
  188.9 5.3 %copy-start.18 = (f32[128,2048]{1,0:T(8,128)}, f32[128,2048]{1,0:T(8,128)S(1)}, u32[]{:S(2)}) copy-start(f32[128,2048]{1,0:T(8,128)S(1)} %get-tuple-element.136) | copy-start | bytes 3145732
  189.0 5.3 %copy-start.38 = (f32[128]{0:T(128)}, f32[128]{0:T(128)S(1)}, u32[]{:S(2)}) copy-start(f32[128]{0:T(128)S(1)} %add_rsqrt_fusion.3) | copy-start | bytes 1540
  233.9 9.8 %copy-start.47 = (bf16[16,64,2048]{2,1,0:T(8,128)(2,1)S(1)}, bf16[16,64,2048]{2,1,0:T(8,128)(2,1)}, u32[]{:S(2)}) copy-start(bf16[16,64,2048]{2,1,0:T(8,128)(2,1)} %get-tuple-element.44) | copy-start | bytes 12582916
  249.3 8.8 %slice-start.2 = ((s8[6291456]{0:T(1024)(128)(4,1)}), s8[4194304]{0:T(1024)(128)(4,1)S(1)}, s32[]{:S(2)}) async-start(s8[6291456]{0:T(1024)(128)(4,1)} %bitcast.222), calls=%async_computation.2 | async-start | bytes 8388608
  274.7 31.2 %slice-start = ((s8[8388608]{0:T(1024)(128)(4,1)}), s8[4194304]{0:T(1024)(128)(4,1)S(1)}, s32[]{:S(2)}) async-start(s8[8388608]{0:T(1024)(128)(4,1)} %bitcast.197), calls=%async_computation | async-start | bytes 8388608
  275.1 30.0 %copy-start.19 = (f32[128,2048]{1,0:T(8,128)S(1)}, f32[128,2048]{1,0:T(8,128)}, u32[]{:S(2)}) copy-start(f32[128,2048]{1,0:T(8,128)} %copy-done.18) | copy-start | bytes 3145732
  275.1 30.0 %copy-start.34 = (f32[2048]{0:T(1024)S(1)}, f32[2048]{0:T(1024)}, u32[]{:S(2)}) copy-start(f32[2048]{0:T(1024)} %param.21) | copy-start | bytes 24580
  275.1 30.0 %copy-start.39 = (f32[128]{0:T(128)S(1)}, f32[128]{0:T(128)}, u32[]{:S(2)}) copy-start(f32[128]{0:T(128)} %copy-done.38) | copy-start | bytes 1540
  275.1 30.4 %copy-start.26 = (bf16[1,2,1,64,2048]{4,3,2,1,0:T(8,128)(2,1)S(1)}, bf16[1,2,1,64,2048]{4,3,2,1,0:T(8,128)(2,1)}, u32[]{:S(2)}) copy-start(bf16[1,2,1,64,2048]{4,3,2,1,0:T(8,128)(2,1)} %param.25) | copy-start | bytes 1572868
  275.1 30.7 %slice-start.1 = ((s8[8388608]{0:T(1024)(128)(4,1)}), s8[4194304]{0:T(1024)(128)(4,1)S(1)}, s32[]{:S(2)}) async-start(s8[8388608]{0:T(1024)(128)(4,1)} %bitcast.197), calls=%async_computation.1 | async-start | bytes 8388608
  315.7 68.6 %copy-start.9 = (f32[1024,128]{1,0:T(8,128)S(1)}, f32[1024,128]{1,0:T(8,128)}, u32[]{:S(2)}) copy-start(f32[1024,128]{1,0:T(8,128)} %copy-done.8) | copy-start | bytes 1572868
  410.3 32.0 %copy-start.4 = (bf16[1,2,1,64,2048]{4,3,2,1,0:T(8,128)(2,1)S(1)}, bf16[1,2,1,64,2048]{4,3,2,1,0:T(8,128)(2,1)}, u32[]{:S(2)}) copy-start(bf16[1,2,1,64,2048]{4,3,2,1,0:T(8,128)(2,1)} %param.13) | copy-start | bytes 1572868
  410.3 32.0 %copy-start.41 = (f32[2,64]{1,0:T(2,128)S(1)}, f32[2,64]{1,0:T(2,128)}, u32[]{:S(2)}) copy-start(f32[2,64]{1,0:T(2,128)} %copy-done.40) | copy-start | bytes 1540
  410.3 32.4 %copy-start.31 = (bf16[128,1536]{1,0:T(8,128)(2,1)S(1)}, bf16[128,1536]{1,0:T(8,128)(2,1)}, u32[]{:S(2)}) copy-start(bf16[128,1536]{1,0:T(8,128)(2,1)} %get-tuple-element.58) | copy-start | bytes 1179652
  442.3 20.4 %copy-start.12 = (f32[2,64,2048]{2,1,0:T(8,128)}, f32[2,64,2048]{2,1,0:T(8,128)S(1)}, u32[]{:S(2)}) copy-start(f32[2,64,2048]{2,1,0:T(8,128)S(1)} %get-tuple-element.57) | copy-start | bytes 3145732
  461.3 7.0 %copy-start.35 = (f32[2048]{0:T(1024)S(1)}, f32[2048]{0:T(1024)}, u32[]{:S(2)}) copy-start(f32[2048]{0:T(1024)} %param.21) | copy-start | bytes 24580
  (32 other events, 100.2 us)
